TPU v7x, 256 devices: a whole 4x4x8 slice. The times are simulated.
256 devices in a mesh: group: 32 (over z, x), member: 8 (over y, core).
Axes of the slice: x: 4, y: 4, z: 8, core: 2. Of those that a mesh axis runs over, the one named last changes fastest.
Arguments:
- node_latent: bfloat16 [131072, 128], P(('group', 'member')), may hold values from -6 to 6
- edge_latent: bfloat16 [786432, 128], P(('group', 'member')), may hold values from -6 to 6
- edge_src: int32 [786432], P(('group', 'member')), may hold values from 0 to 767
- edge_dst: int32 [786432], P(('group', 'member')), may hold values from 0 to 511
- edge_count: int32 [256], P(('group', 'member')), may hold values from 1536 to 3072, as said below
- halo_send: int32 [256, 2, 128], P(('group', 'member')), may hold values from 0 to 511
- halo_count: int32 [256, 2], P(('group', 'member')), may hold values from 64 to 128, as said below
- pool_index: int32 [131072], P(('group', 'member')), may hold values from 0 to 255, as said below
- coarse_src: int32 [49152], P('group'), may hold values from 0 to 511
- coarse_dst: int32 [49152], P('group'), may hold values from 0 to 255
- coarse_count: int32 [32], P('group'), may hold values from 768 to 1536, as said below
- coarse_send: int32 [32, 2, 128], P('group'), may hold values from 0 to 255
- coarse_halo_count: int32 [32, 2], P('group'), may hold values from 64 to 128, as said below
- w_edge_in: bfloat16 [384, 128], replicated, may hold values from -0.3125 to 0.3125
- w_node_in: bfloat16 [256, 128], replicated, may hold values from -0.375 to 0.375
- w_cedge_in: bfloat16 [256, 128], replicated, may hold values from -0.375 to 0.375
- w_cnode_in: bfloat16 [256, 128], replicated, may hold values from -0.375 to 0.375
- w_outs: bfloat16 [5, 128, 128], replicated, may hold values from -0.5 to 0.5
- cot_nodes: bfloat16 [131072, 128], P(('group', 'member')), may hold values from -24 to 24
- cot_edges: bfloat16 [786432, 128], P(('group', 'member')), may hold values from -6 to 6
Outputs:
- new_nodes: bfloat16 [131072, 128], P(('group', 'member'))
- new_edges: bfloat16 [786432, 128], P(('group', 'member'))
- grad_nodes: bfloat16 [131072, 128], P(('group', 'member'))
- grad_edges: bfloat16 [786432, 128], P(('group', 'member'))
- grad_edge_in: float32 [384, 128], replicated
- grad_node_in: float32 [256, 128], replicated
- grad_cedge_in: float32 [256, 128], replicated
- grad_cnode_in: float32 [256, 128], replicated
- grad_outs: float32 [5, 128, 128], replicated
Inputs may be any that keep to these rules, and one draw needn't show every extreme that they name: `edge_count`: in every draw some fine partition has all 3072 edge rows live. `halo_count`: in every draw some send list is full. `pool_index`: every coarse node of a coarse partition receives at least one fine node of that partition. `coarse_count`: in every draw some coarse partition has all 1536 edge rows live. `coarse_halo_count`: in every draw some coarse send list is full.
All inputs are finite; a program needn't handle non-finite values.
Results may differ from a plain program's by a relative error of at most 0.022.
Values may be sent and summed in bfloat16 or wider, within the bound.
No kernel may reach another device: no remote copies, remote signals or barrier semaphores. Data moves between devices by JAX's collectives and lax.ppermute only.
A program may use at most 64 MiB of HBM per device.

v0:
```python
import functools

import jax
import jax.numpy as jnp
from jax import lax
from jax.experimental import pallas as pl
from jax.experimental.pallas import tpu as pltpu
from jax.sharding import Mesh
from jax.sharding import PartitionSpec as P

F32 = jnp.float32
BF = jnp.bfloat16
I32 = jnp.int32
EPS = 1e-05

L = 128
NF = 512
EF = 3072
NC = 256
EC = 1536
SLOT = 128
FINE_BLK = 8
COARSE_BLK = 12
CNT = 16
PART = 272
GRADS = 1792
ROWS_EDGE, ROWS_NODE, ROWS_CEDGE, ROWS_CNODE, ROWS_OUTS = 0, 384, 640, 896, 1152

EVERY = ("z", "x", "y", "c")
GROUP = ("z", "x")
PLANE = ("x", "y", "c")

VMEM = pl.BlockSpec(memory_space=pltpu.VMEM)
HBM = pl.BlockSpec(memory_space=pltpu.HBM)
SMEM = pl.BlockSpec(memory_space=pltpu.SMEM)


def call(kernel, name, out_shape, ins, flops=10**9, space=VMEM, hbm_out=(), scratch=()):
    size = sum(a.size * a.dtype.itemsize for a in ins)
    outs = out_shape if isinstance(out_shape, tuple) else (out_shape,)
    specs = tuple(HBM if k in hbm_out else VMEM for k in range(len(outs)))
    return pl.pallas_call(
        kernel,
        name=name,
        out_shape=out_shape,
        in_specs=[space] * len(ins),
        out_specs=specs if isinstance(out_shape, tuple) else specs[0],
        scratch_shapes=scratch,
        cost_estimate=pl.CostEstimate(flops=flops, bytes_accessed=size, transcendentals=0),
        compiler_params=pltpu.CompilerParams(vmem_limit_bytes=32 * 2**20),
    )(*ins)


def shape(*dims, dtype=BF):
    return jax.ShapeDtypeStruct(dims, dtype)


def dot(a, b):
    return jnp.dot(a, b, preferred_element_type=F32)


def dot_nt(a, b):
    return lax.dot_general(a, b, (((1,), (1,)), ((), ())), preferred_element_type=F32)


def dot_tn(a, b):
    return lax.dot_general(a, b, (((0,), (0,)), ((), ())), preferred_element_type=F32)


def mean(v):
    return jnp.mean(v, axis=-1, keepdims=True)


def columns(rows):
    pad = -rows.shape[0] % 8
    rows = rows.astype(F32)
    if pad:
        rows = jnp.concatenate([rows, jnp.zeros((pad, 128), F32)], 0)
    return rows.T.astype(I32)


def pick(cols, blocks, n):
    lane = lax.broadcasted_iota(I32, (128, n), 1)
    return jnp.concatenate(
        [jnp.where(lane == cols[:, j : j + 1], 1.0, 0.0).astype(BF) for j in blocks], 0
    )


def put(rows, blocks, n):
    line = lax.broadcasted_iota(I32, (n, 128), 0)
    return jnp.concatenate(
        [jnp.where(line == rows[j : j + 1, :], 1.0, 0.0).astype(BF) for j in blocks], 1
    )


def live_rows(rows, count):
    at = lax.broadcasted_iota(I32, rows.shape, 0) * 128 + lax.broadcasted_iota(I32, rows.shape, 1)
    return jnp.where(at < jnp.broadcast_to(count, rows.shape), rows, -1)


def live_slots(send, counts, axes):
    spot, last = 0, 1
    for axis in axes:
        spot = spot * lax.axis_size(axis) + lax.axis_index(axis)
        last = last * lax.axis_size(axis)
    there = ((spot > 0).astype(I32), (spot < last - 1).astype(I32))
    lane = lax.broadcasted_iota(I32, (1, SLOT), 1)
    return jnp.concatenate(
        [
            jnp.where(
                lane < jnp.broadcast_to(counts[0:1, s : s + 1], (1, SLOT)) * there[s],
                send[s : s + 1, :],
                -1,
            )
            for s in (0, 1)
        ],
        0,
    )


def sigmoid(a):
    return 1.0 / (1.0 + jnp.exp(-a))


def normed_of(hidden, w_second):
    outcome = dot(hidden, w_second)
    centred = outcome - mean(outcome)
    inv = lax.rsqrt(mean(centred * centred) + EPS)
    return centred * inv, inv


def activation(a):
    sig = sigmoid(a)
    return (a * sig).astype(BF), sig * (1.0 + a * (1.0 - sig))


def norm_back(grad, normed, inv):
    return (inv * (grad - mean(grad) - normed * mean(grad * normed))).astype(BF)


def forward(a, w_second):
    return normed_of((a * sigmoid(a)).astype(BF), w_second)[0]


def begin_kernel(live, clive, out):
    at = lax.broadcasted_iota(I32, out.shape, 0)
    out[...] = jnp.where(at == 0, live[0], jnp.where(at == 1, clive[0], 0))


def send_kernel(lives, node, send, counts, to_prev, to_next):
    cols = columns(live_slots(send[...] + lives[2:4, :], counts, EVERY))
    rows = node[...]
    to_prev[...] = dot(pick(cols, (0,), NF), rows).astype(BF)
    to_next[...] = dot(pick(cols, (1,), NF), rows).astype(BF)


def pre_kernel(node, w_in, src, dst, edge, pool, cot, pre, side, src_rows, dst_rows):
    w = w_in[...]
    rows = node[...]
    src_table = jnp.concatenate([dot(rows, w[128:256]).astype(BF), rows], 1)
    dst_table = jnp.concatenate([dot(rows, w[256:384]).astype(BF), rows], 1)
    src_cols, dst_cols = columns(src[...]), columns(dst[...])
    for c in range(EF // 128 // FINE_BLK):
        blocks = range(c * FINE_BLK, (c + 1) * FINE_BLK)
        at = pl.ds(c * FINE_BLK * 128, FINE_BLK * 128)
        from_src = dot(pick(src_cols, blocks, NF), src_table)
        from_dst = dot(pick(dst_cols, blocks, NF), dst_table)
        pre[at, :] = dot(edge[at, :], w[:128]) + from_src[:, :L] + from_dst[:, :L]
        src_rows[at, :] = from_src[:, L:].astype(BF)
        dst_rows[at, :] = from_dst[:, L:].astype(BF)
    pool_hot = put(pool[...], range(NF // 128), NC)
    side[0:NC, :] = dot(pool_hot, cot[...]).astype(BF)
    count = dot_nt(jnp.ones((8, NF), BF), pool_hot)
    high = jnp.floor(count * (1.0 / 16.0))
    low = count - 16.0 * high
    at = lax.broadcasted_iota(I32, (CNT, 128), 0)
    lines = jnp.zeros((CNT, 128), F32)
    for k, v in enumerate((high[0:1, :128], high[0:1, 128:], low[0:1, :128], low[0:1, 128:])):
        lines = jnp.where(at == k, v, lines)
    side[NC : NC + CNT, :] = lines.astype(BF)


def fine_kernel(
    live, pre, edge, node, from_prev, from_next, src, dst, w_in, w_node, w_outs, pool, side,
    new_edges_hbm, act, agg_out, act_node, refined, payload, new_edges, sems,
):
    halo = jnp.concatenate([from_prev[...], from_next[...]], 0)
    table = dot(halo, w_in[128:256, :]).astype(BF)
    src_cols = columns(src[...] - NF)
    dst_rows = live_rows(dst[...], live[0:1, 0:1])
    w_second = w_outs[0]
    total = jnp.zeros((NF, L), F32)
    copies = []
    for c in range(EF // 128 // FINE_BLK):
        blocks = range(c * FINE_BLK, (c + 1) * FINE_BLK)
        at = pl.ds(c * FINE_BLK * 128, FINE_BLK * 128)
        a = pre[at, :] + dot(pick(src_cols, blocks, 2 * SLOT), table)
        act[at, :] = a
        message = forward(a, w_second)
        here = lax.broadcasted_iota(I32, message.shape, 0) + c * FINE_BLK * 128
        here = here < jnp.broadcast_to(live[0:1, 0:1], message.shape)
        rows = (edge[at, :].astype(F32) + jnp.where(here, message, 0.0)).astype(BF)
        new_edges[at, :] = rows
        copies.append(pltpu.make_async_copy(new_edges.at[at], new_edges_hbm.at[at], sems.at[c]))
        copies[-1].start()
        total += dot(put(dst_rows, blocks, NF), rows)
    agg = total.astype(BF)
    agg_out[...] = agg
    a = dot(node[...], w_node[:128, :]) + dot(agg, w_node[128:, :])
    act_node[...] = a
    rows = (node[...].astype(F32) + forward(a, w_outs[1])).astype(BF)
    refined[...] = rows
    payload[0:NC, :] = dot(put(pool[...], range(NF // 128), NC), rows).astype(BF)
    payload[NC:, :] = side[...]
    for copy in copies:
        copy.wait()


def pair_kernel(a, b, out, part):
    out[...] = (a[...].astype(F32) + b[...].astype(F32)).astype(BF)
    part[...] = out[pl.ds(pl.multiple_of(lax.axis_index("c") * NC, NC), PART), :]


def join_kernel(own, near, part, ahead, out, total):
    core = lax.axis_index("c")
    total[...] = near[...].astype(F32) + jnp.where(core == 0, own[...].astype(F32), 0.0)
    line = lax.broadcasted_iota(I32, (PART, L), 0)
    rows = jnp.where(line < NC + core * PART, part[...].astype(F32), 0.0)
    at = pl.ds(pl.multiple_of(core * NC, NC), PART)
    total[at, :] = total[at, :] + rows
    out[...] = total[...].astype(BF)


def pool_kernel(a, b, send, counts, own_out, cot_out, divisor, to_prev, to_next):
    total = a[...].astype(F32) + b[...].astype(F32)
    lines = total[2 * NC :, :]
    count = 16.0 * lines[0:2, :] + lines[2:4, :]
    cols = jnp.concatenate([count, jnp.ones((6, 128), F32)], 0).T
    count = jnp.concatenate(
        [jnp.broadcast_to(cols[:, k : k + 1], (128, L)) for k in (0, 1)], 0
    )
    own = (total[:NC, :] / count).astype(BF)
    own_out[...] = own
    cot_out[...] = total[NC : 2 * NC, :].astype(BF)
    divisor[...] = count
    cols = columns(live_slots(send[...], counts, GROUP))
    to_prev[...] = dot(pick(cols, (0,), NC), own).astype(BF)
    to_next[...] = dot(pick(cols, (1,), NC), own).astype(BF)


def coarse_pre_kernel(own, cot, src, dst, w_in, w_node, w_outs, pre, pre_node, grad_coarse):
    rows = own[...]
    table = jnp.concatenate([dot(rows, w_in[128:, :]), dot(rows, w_in[:128, :])], 0).astype(BF)
    src_cols, dst_cols = columns(src[...]), columns(dst[...])
    for c in range(EC // 128 // COARSE_BLK):
        blocks = range(c * COARSE_BLK, (c + 1) * COARSE_BLK)
        hot = jnp.concatenate([pick(dst_cols, blocks, NC), pick(src_cols, blocks, NC)], 1)
        pre[pl.ds(c * COARSE_BLK * 128, COARSE_BLK * 128), :] = dot(hot, table)
    pre_node[...] = dot(rows, w_node[:128, :])
    grad_coarse[...] = dot_nt(cot[...], w_outs[4]).astype(BF)


def coarse_kernel(
    live, own, pre, pre_node, grad_coarse, from_prev, from_next, src, dst, w_in, w_node, w_outs,
    coarse_out, grad_own, back_prev, back_next, sums_out, agg_out, ga_out, pair_node, pair_edge, ga_edge,
):
    halo = jnp.concatenate([from_prev[...], from_next[...]], 0)
    table = dot(halo, w_in[:128, :]).astype(BF)
    blocks = range(EC // 128)
    src_rows = src[...]
    dst_rows = live_rows(dst[...], live[1:2, 0:1])
    a = pre[...] + dot(pick(columns(src_rows - NC), blocks, 2 * SLOT), table)
    hidden, slope = activation(a)
    normed, inv = normed_of(hidden, w_outs[2])
    put_dst = put(dst_rows, blocks, NC)
    agg = dot(put_dst, normed.astype(BF)).astype(BF)
    agg_out[...] = agg
    a = pre_node[...] + dot(agg, w_node[128:, :])
    hidden_node, slope_node = activation(a)
    normed_node, inv_node = normed_of(hidden_node, w_outs[3])
    coarse_out[...] = (own[...].astype(F32) + normed_node).astype(BF)
    grad = grad_coarse[...].astype(F32)
    go = norm_back(grad, normed_node, inv_node)
    ga = (dot_nt(go, w_outs[3]) * slope_node).astype(BF)
    ga_out[...] = ga
    pair_node[0] = hidden_node
    pair_node[1] = go
    grad_total = grad + dot_nt(ga, w_node[:128, :])
    grad_agg = dot_nt(ga, w_node[128:, :]).astype(BF)
    grad = dot(pick(columns(dst_rows), blocks, NC), grad_agg)
    go = norm_back(grad, normed, inv)
    pair_edge[0] = hidden
    pair_edge[1] = go
    ga = (dot_nt(go, w_outs[2]) * slope).astype(BF)
    src_sums = dot(put(src_rows, blocks, NC + 2 * SLOT), ga).astype(BF)
    sums_out[...] = src_sums
    ga_edge[...] = ga
    grad_ext = dot_nt(src_sums, w_in[:128, :])
    back_prev[...] = grad_ext[NC : NC + SLOT].astype(BF)
    back_next[...] = grad_ext[NC + SLOT :].astype(BF)
    grad_own[...] = grad_total + grad_ext[:NC]


def lift_kernel(
    own, cot, from_prev, from_next, coarse, grad_part, sums, agg, ga, pair_node, pair_edge,
    ga_edge, dst, w_in, refined, pool, w_outs, new_nodes, grads, grad_own,
):
    part = 1.0 / 8.0
    rows = own[...]
    ext = jnp.concatenate([rows, from_prev[...], from_next[...]], 0)
    dst_sums = dot(put(dst[...], range(EC // 128), NC), ga_edge[...]).astype(BF)
    grad_own[...] = grad_part[...] + dot_nt(dst_sums, w_in[128:, :])
    lifted = dot(pick(columns(pool[...]), range(NF // 128), NC), coarse[...]).astype(BF)
    new_nodes[...] = (refined[...].astype(F32) + dot(lifted, w_outs[4])).astype(BF)
    grads[0:128, :] = (part * dot_tn(ext, sums[...])).astype(BF)
    grads[128:256, :] = (part * dot_tn(rows, dst_sums)).astype(BF)
    grads[256:384, :] = (part * dot_tn(rows, ga[...])).astype(BF)
    grads[384:512, :] = (part * dot_tn(agg[...], ga[...])).astype(BF)
    grads[512:640, :] = (part * dot_tn(pair_edge[0], pair_edge[1])).astype(BF)
    grads[640:768, :] = (part * dot_tn(pair_node[0], pair_node[1])).astype(BF)
    grads[768:896, :] = (part * dot_tn(coarse[...], cot[...])).astype(BF)


def prep_kernel(
    act, act_node, w_outs, src, from_prev, from_next, src_part, src_rows, hidden_out, slope_out, normed_out, inv_out, hidden_node, slope_node,
    normed_node, inv_node,
):
    halo = jnp.concatenate([from_prev[...], from_next[...]], 0)
    src_cols = columns(src[...] - NF)
    for c in range(EF // 128 // FINE_BLK):
        at = pl.ds(c * FINE_BLK * 128, FINE_BLK * 128)
        blocks = range(c * FINE_BLK, (c + 1) * FINE_BLK)
        src_rows[at, :] = src_part[at, :] + dot(pick(src_cols, blocks, 2 * SLOT), halo).astype(BF)
        hidden, slope = activation(act[at, :])
        normed, inv = normed_of(hidden, w_outs[0])
        hidden_out[at, :] = hidden
        slope_out[at, :] = slope.astype(BF)
        normed_out[at, :] = normed.astype(BF)
        inv_out[at, :] = inv
    hidden, slope = activation(act_node[...])
    normed, inv = normed_of(hidden, w_outs[1])
    hidden_node[...] = hidden
    slope_node[...] = slope
    normed_node[...] = normed
    inv_node[...] = inv


def fine_back_kernel(
    lives, counts, grad_own, divisor, ret_prev, ret_next, send, cot, pool, node, agg, src_rows,
    hidden, slope, normed, inv, hidden_node, slope_node, normed_node, inv_node, dst_rows, edge,
    cot_edges, src, dst, w_in, w_node, w_outs, coarse_grads, grad_new, ga_out, grad_node, grads,
    back_prev, back_next,
):
    back = jnp.concatenate([ret_prev[...], ret_next[...]], 0)
    hot = put(live_slots(send[...], counts, GROUP), (0, 1), NC)
    grad_pool = (grad_own[...] + dot(hot, back)).astype(BF).astype(F32) / divisor[...]
    pooled = dot(pick(columns(pool[...]), range(NF // 128), NC), grad_pool.astype(BF))
    grad_refined = (cot[...].astype(F32) + pooled).astype(BF).astype(F32)
    go = norm_back(grad_refined, normed_node[...], inv_node[...])
    ga = (dot_nt(go, w_outs[1]) * slope_node[...]).astype(BF)
    grad_agg = dot_nt(ga, w_node[128:, :]).astype(BF)
    grads[384:512, :] = dot_tn(node[...], ga).astype(BF)
    grads[512:640, :] = dot_tn(agg[...], ga).astype(BF)
    grads[1280:1408, :] = dot_tn(hidden_node[...], go).astype(BF)
    grad_node[...] = grad_refined + dot_nt(ga, w_node[:128, :])
    dst_cols = columns(live_rows(dst[...], lives[0:1, 0:1]))
    slot_rows = src[...] - NF
    sums = jnp.zeros((2 * SLOT, L), F32)
    w_second = w_outs[0]
    totals = [jnp.zeros((L, L), F32) for _ in range(4)]
    for c in range(EF // 128 // FINE_BLK):
        blocks = range(c * FINE_BLK, (c + 1) * FINE_BLK)
        at = pl.ds(c * FINE_BLK * 128, FINE_BLK * 128)
        gathered = dot(pick(dst_cols, blocks, NF), grad_agg)
        total = (cot_edges[at, :].astype(F32) + gathered).astype(BF)
        grad_new[at, :] = total
        here = lax.broadcasted_iota(I32, total.shape, 0) + c * FINE_BLK * 128
        here = here < jnp.broadcast_to(lives[0:1, 0:1], total.shape)
        total = jnp.where(here, total.astype(F32), 0.0)
        go = norm_back(total, normed[at, :].astype(F32), inv[at, :])
        ga = (dot_nt(go, w_second) * slope[at, :].astype(F32)).astype(BF)
        ga_out[at, :] = ga
        sums += dot(put(slot_rows, blocks, 2 * SLOT), ga)
        for k, rows in enumerate((edge, src_rows, dst_rows)):
            totals[k] += dot_tn(rows[at, :], ga)
        totals[3] += dot_tn(hidden[at, :], go)
    sums = dot_nt(sums.astype(BF), w_in[128:256, :])
    back_prev[...] = sums[:SLOT].astype(BF)
    back_next[...] = sums[SLOT:].astype(BF)
    for k in range(3):
        grads[k * 128 : (k + 1) * 128, :] = totals[k].astype(BF)
    grads[640:1152, :] = coarse_grads[0:512, :]
    grads[1152:1280, :] = totals[3].astype(BF)
    grads[1408:1792, :] = coarse_grads[512:896, :]


def fine_rest_kernel(
    counts, grad_new, ga, grad_part, src, dst, w_in, ret_prev, ret_next, send, grad_edges_hbm,
    grad_nodes, grad_edges, sems,
):
    src_rows, dst_rows = src[...], dst[...]
    src_sums = jnp.zeros((NF, L), F32)
    dst_sums = jnp.zeros((NF, L), F32)
    copies = []
    for c in range(EF // 128 // FINE_BLK):
        blocks = range(c * FINE_BLK, (c + 1) * FINE_BLK)
        at = pl.ds(c * FINE_BLK * 128, FINE_BLK * 128)
        rows = ga[at, :]
        grad_edges[at, :] = (
            grad_new[at, :].astype(F32) + dot_nt(rows, w_in[:128, :])
        ).astype(BF)
        copies.append(pltpu.make_async_copy(grad_edges.at[at], grad_edges_hbm.at[at], sems.at[c]))
        copies[-1].start()
        src_sums += dot(put(src_rows, blocks, NF), rows)
        dst_sums += dot(put(dst_rows, blocks, NF), rows)
    back = jnp.concatenate([ret_prev[...], ret_next[...]], 0)
    hot = put(live_slots(send[...], counts, EVERY), (0, 1), NF)
    grad_nodes[...] = (
        grad_part[...]
        + dot_nt(src_sums.astype(BF), w_in[128:256, :])
        + dot_nt(dst_sums.astype(BF), w_in[256:, :])
        + dot(hot, back)
    ).astype(BF)
    for copy in copies:
        copy.wait()


def added(parts):
    total = parts[0].astype(F32)
    for k in range(1, parts.shape[0]):
        total += parts[k].astype(F32)
    return total.astype(BF)


def plane_kernel(parts, ret_prev, ret_next, out):
    total = added(parts)
    for k in range(out.shape[0]):
        out[k] = total


def spread_kernel(parts, out):
    total = added(parts)
    for k in range(out.shape[0]):
        out[k] = total


def end_kernel(rows, edge_in, node_in, cedge_in, cnode_in, outs):
    edge_in[...] = rows[ROWS_EDGE:ROWS_NODE, :].astype(F32)
    node_in[...] = rows[ROWS_NODE:ROWS_CEDGE, :].astype(F32)
    cedge_in[...] = rows[ROWS_CEDGE:ROWS_CNODE, :].astype(F32)
    cnode_in[...] = rows[ROWS_CNODE:ROWS_OUTS, :].astype(F32)
    for k in range(5):
        outs[k] = rows[ROWS_OUTS + k * 128 : ROWS_OUTS + (k + 1) * 128, :].astype(F32)


def shift(value, axes, step):
    count = lax.axis_size(axes)
    return lax.ppermute(value, axes, [(i, (i + step) % count) for i in range(count)])


def cross(value):
    size = {axis: lax.axis_size(axis) for axis in EVERY}
    count = size["z"] * size["x"] * size["y"] * size["c"]
    pairs = []
    for i in range(count):
        core, y = i % size["c"], i // size["c"] % size["y"]
        to = (y + 1 - 2 * core) % size["y"]
        pairs.append((i, i + (to - y) * size["c"]))
    return lax.ppermute(value, EVERY, pairs)


def exchange(value, axes):
    return lax.all_to_all(value, axes, 0, 0)


def on_device(
    node, edge, src, dst, live, send, counts, pool, csrc, cdst, clive, csend, ccounts,
    w_edge, w_node, w_cedge, w_cnode, w_outs, cot, cot_edges,
):
    f32 = functools.partial(shape, dtype=F32)
    slots = (shape(SLOT, L), shape(SLOT, L))
    src, dst = src.reshape(EF // 128, 128), dst.reshape(EF // 128, 128)
    csrc, cdst = csrc.reshape(EC // 128, 128), cdst.reshape(EC // 128, 128)
    pool = pool.reshape(NF // 128, 128)
    send, csend = send.reshape(2, SLOT), csend.reshape(2, SLOT)
    edge_copies = (pltpu.VMEM((EF, L), BF), pltpu.SemaphoreType.DMA((EF // 128 // FINE_BLK,)))

    lives = call(
        begin_kernel, "begin", shape(8, 128, dtype=I32), (live, clive), 10**10, space=SMEM
    )
    to_prev, to_next = call(send_kernel, "send", slots, (lives, node, send, counts), 10**10)
    from_prev, from_next = shift(to_next, EVERY, 1), shift(to_prev, EVERY, -1)
    pre, side, src_part, dst_rows = call(
        pre_kernel, "pre", (f32(EF, L), shape(NC + CNT, L), shape(EF, L), shape(EF, L)),
        (node, w_edge, src, dst, edge, pool, cot),
    )
    new_edges, act, agg, act_node, refined, payload = call(
        fine_kernel, "fine",
        (shape(EF, L), f32(EF, L), shape(NF, L), f32(NF, L), shape(NF, L), shape(2 * NC + CNT, L)),
        (lives, pre, edge, node, from_prev, from_next, src, dst, w_edge, w_node, w_outs, pool, side),
        hbm_out=(0,), scratch=edge_copies,
    )
    total, part = call(
        pair_kernel, "pair", (shape(2 * NC + CNT, L), shape(PART, L)),
        (payload, shift(payload, "c", 1)), 10**6,
    )
    near, part = cross(total), shift(part, "y", 2)
    prepared = call(
        prep_kernel, "prep",
        (shape(EF, L), shape(EF, L), shape(EF, L), shape(EF, L), f32(EF, 1),
         shape(NF, L), f32(NF, L), f32(NF, L), f32(NF, 1)),
        (act, act_node, w_outs, src, from_prev, from_next, src_part),
    )
    joined = call(
        join_kernel, "join", shape(2 * NC + CNT, L), (total, near, part, prepared[-1]), 10**6,
        scratch=(pltpu.VMEM((2 * NC + CNT, L), F32),),
    )
    own, pooled_cot, divisor, to_prev, to_next = call(
        pool_kernel, "pool", (shape(NC, L), shape(NC, L), f32(NC, L)) + slots,
        (joined, shift(joined, "c", 1), csend, ccounts), 10**7,
    )
    cfrom_prev, cfrom_next = shift(to_next, GROUP, 1), shift(to_prev, GROUP, -1)
    cpre, cpre_node, grad_coarse = call(
        coarse_pre_kernel, "coarse_pre", (f32(EC, L), f32(NC, L), shape(NC, L)),
        (own, pooled_cot, csrc, cdst, w_cedge, w_cnode, w_outs),
    )
    coarse, grad_part, back_prev, back_next, sums, cagg, cga, pair_node, pair_edge, cga_edge = call(
        coarse_kernel, "coarse",
        (shape(NC, L), f32(NC, L)) + slots
        + (shape(NC + 2 * SLOT, L), shape(NC, L), shape(NC, L), shape(2, NC, L),
           shape(2, EC, L), shape(EC, L)),
        (lives, own, cpre, cpre_node, grad_coarse, cfrom_prev, cfrom_next, csrc, cdst,
         w_cedge, w_cnode, w_outs),
    )
    cret_prev, cret_next = shift(back_next, GROUP, 1), shift(back_prev, GROUP, -1)
    new_nodes, coarse_grads, grad_own = call(
        lift_kernel, "lift", (shape(NF, L), shape(896, L), f32(NC, L)),
        (own, pooled_cot, cfrom_prev, cfrom_next, coarse, grad_part, sums, cagg, cga, pair_node,
         pair_edge, cga_edge, cdst, w_cedge, refined, pool, w_outs),
    )
    grad_new, ga, grad_part, grads, back_prev, back_next = call(
        fine_back_kernel, "fine_back",
        (shape(EF, L), shape(EF, L), f32(NF, L), shape(GRADS, L)) + slots,
        (lives, ccounts, grad_own, divisor, cret_prev, cret_next, csend, cot, pool, node, agg)
        + tuple(prepared)
        + (dst_rows, edge, cot_edges, src, dst, w_edge, w_node, w_outs, coarse_grads),
    )
    ret_prev, ret_next = shift(back_next, EVERY, 1), shift(back_prev, EVERY, -1)
    parts = exchange(grads.reshape(32, GRADS // 32, L), PLANE)
    spread = call(
        plane_kernel, "sum_plane", shape(8, GRADS // 32, L), (parts, ret_prev, ret_next), 10**6
    )
    grad_edges, grad_nodes = call(
        fine_rest_kernel, "fine_rest", (shape(EF, L), shape(NF, L)),
        (counts, grad_new, ga, grad_part, src, dst, w_edge, ret_prev, ret_next, send),
        hbm_out=(0,), scratch=edge_copies,
    )
    parts = exchange(spread, "z")
    spread = call(spread_kernel, "sum_z", shape(32, GRADS // 32, L), (parts,), 10**6)
    rows = exchange(spread, PLANE).reshape(GRADS, L)
    weights = call(
        end_kernel, "end", (f32(384, L), f32(256, L), f32(256, L), f32(256, L), f32(5, L, L)),
        (rows,), 10**6,
    )
    return (new_nodes, new_edges, grad_nodes, grad_edges) + tuple(weights)


def solution(mesh):
    cube = Mesh(mesh.devices.reshape(8, 4, 4, 2), EVERY)
    fine, coarse = P(EVERY), P(GROUP)
    in_specs = (fine,) * 8 + (coarse,) * 5 + (P(),) * 5 + (fine,) * 2
    out_specs = (fine,) * 4 + (P(),) * 5
    return jax.shard_map(
        on_device, mesh=cube, in_specs=in_specs, out_specs=out_specs, check_vma=False
    )
```

profile of v0, /device:TPU:1, one launch (start us, length us, event | category | flops | bytes accessed | tf_op | source)
XLA Modules:
  0.0 104.5 jit_solution(7503008597798124865)
XLA Ops:
  1.9 0.0 copy-start.3
  1.9 0.0 copy-start.16
  2.0 0.0 copy-start.17
  2.0 0.9 copy-done.3
  2.9 0.0 copy-start.5
  2.9 0.0 copy-start.7
  2.9 0.0 copy-start.8
  2.9 0.0 copy-start.10
  2.9 0.4 send.1
  3.3 2.8 %collective-permute-start = (bf16[128,128]{1,0:T(8,128)(2,1)S(1)}, bf16[128,128]{1,0:T(8,128)(2,1)S(1)}, u32[]{:S(2)}, u32[]{:S(2)}) collective-permute-start(bf16[128,128]{1,0:T(8,128)(2,1)S(1)} %get-tuple-element.67), channel_id=1, source_target_pairs={{0,1},{1,2},{2,3},{3,4},{4,5},{5,6},{6,7},{7,8},{8,9},{9,10},{10,1... | collective-permute-start | bytes 98312 | tf_op jit(solution)/shard_map/ppermute | solution.py:458
  6.1 0.6 collective-permute-start.1
  6.7 0.0 copy-done.4
  6.8 0.0 copy-start.2
  6.8 0.0 copy-start.6
  6.8 2.3 %pre.1 = (f32[3072,128]{1,0:T(8,128)S(1)}, bf16[272,128]{1,0:T(8,128)(2,1)S(1)}, bf16[3072,128]{1,0:T(8,128)(2,1)S(1)}, bf16[3072,128]{1,0:T(8,128)(2,1)S(1)}) custom-call(bf16[512,128]{1,0:T(8,128)(2,1)S(1)} %copy-done.3, bf16[384,128]{1,0:T(8,128)(2,1)S(1)} %copy-done.5, s32[24,128]{1,0:T(8,128)S(1)} %bitcast.10, s32[24,128]{1,0:T(8,128)S(1)} %bitcast.15, ...), custom_call_target="tpu_custom_call" | custom-call | flops 1000000000 | bytes 1173504 | tf_op jit(solution)/shard_map/pre/pallas_call | solution.py:42
  9.1 0.0 collective-permute-done.from_prev
  9.1 0.3 collective-permute-done.1.from_next
  9.4 3.9 %fine.1 = (bf16[3072,128]{1,0:T(8,128)(2,1)}, f32[3072,128]{1,0:T(8,128)S(1)}, bf16[512,128]{1,0:T(8,128)(2,1)S(1)}, f32[512,128]{1,0:T(8,128)S(1)}, bf16[512,12...) custom-call(s32[8,128]{1,0:T(8,128)S(1)} %begin.1.lives.live, f32[3072,128]{1,0:T(8,128)S(1)} %get-tuple-element.66.pre, ...), custom_call_target="tpu_custom_call" | custom-call | flops 1000000000 | bytes 2983936 | tf_op jit(solution)/shard_map/fine/pallas_call | solution.py:42
  13.4 8.0 %collective-permute-start.2 = (bf16[528,128]{1,0:T(8,128)(2,1)S(1)}, bf16[528,128]{1,0:T(8,128)(2,1)S(1)}, u32[]{:S(2)}, u32[]{:S(2)}) collective-permute-start(bf16[528,128]{1,0:T(8,128)(2,1)S(1)} %get-tuple-element.70.a), channel_id=1, source_target_pairs={{0,1},{1,0},{2,3},{3,2},{4,5},{5,4},{6,7},{7,6},{8,9},{9,8},{10,11... | collective-permute-start | bytes 405512 | tf_op jit(solution)/shard_map/ppermute | solution.py:458
  21.4 1.0 collective-permute-done.2.b
  22.4 0.1 pair.1
  22.4 0.1 collective-permute-start.3
  22.5 0.1 collective-permute-start.4
  22.6 0.0 copy-start.9
  22.6 0.0 copy-start.11
  22.7 0.0 copy-start.12
  22.7 0.0 copy-start.13
  22.7 0.0 copy-start.14
  22.7 0.0 copy-start.15
  22.7 2.0 %prep.1 = (bf16[3072,128]{1,0:T(8,128)(2,1)S(1)}, bf16[3072,128]{1,0:T(8,128)(2,1)S(1)}, bf16[3072,128]{1,0:T(8,128)(2,1)S(1)}, bf16[3072,128]{1,0:T(8,128)(2,1)...) custom-call(f32[3072,128]{1,0:T(8,128)S(1)} %get-tuple-element.73.ac, ...), custom_call_target="tpu_custom_call" | custom-call | flops 1000000000 | bytes 2863104 | tf_op jit(solution)/shard_map/prep/pallas_call | solution.py:42
  24.7 2.6 %collective-permute-done.4.part = bf16[272,128]{1,0:T(8,128)(2,1)S(1)} collective-permute-done((bf16[272,128]{1,0:T(8,128)(2,1)S(1)}, bf16[272,128]{1,0:T(8,128)(2,1)S(1)}, u32[]{:S(2)}, u32[]{:S(2)}) %collective-permute-start.4) | collective-permute-done | bytes 69664 | tf_op jit(solution)/shard_map/ppermute | solution.py:458
  27.3 0.0 collective-permute-done.3.near
  27.3 0.1 join.1.a
  27.4 3.1 %collective-permute-start.5 = (bf16[528,128]{1,0:T(8,128)(2,1)S(1)}, bf16[528,128]{1,0:T(8,128)(2,1)S(1)}, u32[]{:S(2)}, u32[]{:S(2)}) collective-permute-start(bf16[528,128]{1,0:T(8,128)(2,1)S(1)} %join.1.a), channel_id=1, source_target_pairs={{0,1},{1,0},{2,3},{3,2},{4,5},{5,4},{6,7},{7,6},{8,9},{9,8},{10,11... | collective-permute-start | bytes 405512 | tf_op jit(solution)/shard_map/ppermute | solution.py:458
  30.5 1.0 collective-permute-done.5.b
  31.5 0.0 copy-done.9
  31.5 0.4 pool.1
  32.0 0.1 collective-permute-start.6
  32.1 5.4 %collective-permute-start.7 = (bf16[128,128]{1,0:T(8,128)(2,1)S(1)}, bf16[128,128]{1,0:T(8,128)(2,1)S(1)}, u32[]{:S(2)}, u32[]{:S(2)}) collective-permute-start(bf16[128,128]{1,0:T(8,128)(2,1)S(1)} %get-tuple-element.80), channel_id=1, source_target_pairs={{0,248},{8,0},{16,8},{24,16},{32,24},{40,32},{48,40},{56,48},{64,5... | collective-permute-start | bytes 98312 | tf_op jit(solution)/shard_map/ppermute | solution.py:458
  37.5 0.0 copy-done.13
  37.5 0.0 copy-done.15
  37.5 0.9 coarse_pre.1
  38.3 0.3 collective-permute-done.6.from_prev
  38.7 0.0 collective-permute-done.7.from_next
  38.7 3.7 %coarse.1 = (bf16[256,128]{1,0:T(8,128)(2,1)S(1)}, f32[256,128]{1,0:T(8,128)S(1)}, bf16[128,128]{1,0:T(8,128)(2,1)S(1)}, bf16[128,128]{1,0:T(8,128)(2,1)S(1)}, b...) custom-call(s32[8,128]{1,0:T(8,128)S(1)} %begin.1.lives.live, ...), custom_call_target="tpu_custom_call" | custom-call | flops 1000000000 | bytes 1425408 | tf_op jit(solution)/shard_map/coarse/pallas_call | solution.py:42
  42.4 0.1 collective-permute-start.8
  42.5 5.2 %collective-permute-start.9 = (bf16[128,128]{1,0:T(8,128)(2,1)S(1)}, bf16[128,128]{1,0:T(8,128)(2,1)S(1)}, u32[]{:S(2)}, u32[]{:S(2)}) collective-permute-start(bf16[128,128]{1,0:T(8,128)(2,1)S(1)} %get-tuple-element.98), channel_id=1, source_target_pairs={{0,248},{8,0},{16,8},{24,16},{32,24},{40,32},{48,40},{56,48},{64,5... | collective-permute-start | bytes 98312 | tf_op jit(solution)/shard_map/ppermute | solution.py:458
  47.7 1.3 %lift.1 = (bf16[512,128]{1,0:T(8,128)(2,1)}, bf16[896,128]{1,0:T(8,128)(2,1)S(1)}, f32[256,128]{1,0:T(8,128)S(1)}) custom-call(bf16[256,128]{1,0:T(8,128)(2,1)S(1)} %get-tuple-element.77.own, bf16[256,128]{1,0:T(8,128)(2,1)S(1)} %get-tuple-element.78.cot, bf16[128,128]{1,0:T(8,128)(2,1)S(1)} %collective-permute-done.6.from_prev, ...), custom_call_target="tpu_custom_call" | custom-call | flops 1000000000 | bytes 2334720 | tf_op jit(solution)/shard_map/lift/pallas_call | solution.py:42
  49.0 0.0 collective-permute-done.8.ret_prev
  49.0 0.0 collective-permute-done.9.ret_next
  49.0 5.2 %fine_back.1 = (bf16[3072,128]{1,0:T(8,128)(2,1)S(1)}, bf16[3072,128]{1,0:T(8,128)(2,1)S(1)}, f32[512,128]{1,0:T(8,128)S(1)}, bf16[1792,128]{1,0:T(8,128)(2,1)},...) custom-call(s32[8,128]{1,0:T(8,128)S(1)} %begin.1.lives.live, s32[1,2]{1,0:T(1,128)S(1)} %copy-done.11, ...), custom_call_target="tpu_custom_call" | custom-call | flops 1000000000 | bytes 7484424 | tf_op jit(solution)/shard_map/fine_back/pallas_call | solution.py:42
  54.2 5.6 %all-to-all-start = ((bf16[32,56,128]{2,1,0:T(8,128)(2,1)}), bf16[32,56,128]{2,1,0:T(8,128)(2,1)S(1)}, u32[]{:S(2)}, u32[]{:S(2)}) async-start(bf16[32,56,128]{2,1,0:T(8,128)(2,1)} %bitcast.7), calls=%async_computation | async-start | bytes 917504 | tf_op jit(solution)/shard_map/all_to_all | solution.py:473
  59.8 1.7 %collective-permute-start.10 = (bf16[128,128]{1,0:T(8,128)(2,1)S(1)}, bf16[128,128]{1,0:T(8,128)(2,1)S(1)}, u32[]{:S(2)}, u32[]{:S(2)}) collective-permute-start(bf16[128,128]{1,0:T(8,128)(2,1)S(1)} %get-tuple-element.113), channel_id=1, source_target_pairs={{0,1},{1,2},{2,3},{3,4},{4,5},{5,6},{6,7},{7,8},{8,9},{9,10},{10,1... | collective-permute-start | bytes 98312 | tf_op jit(solution)/shard_map/ppermute | solution.py:458
  61.5 0.0 collective-permute-start.11
  61.5 1.2 %collective-permute-done.10.ret_prev = bf16[128,128]{1,0:T(8,128)(2,1)S(1)} collective-permute-done((bf16[128,128]{1,0:T(8,128)(2,1)S(1)}, bf16[128,128]{1,0:T(8,128)(2,1)S(1)}, u32[]{:S(2)}, u32[]{:S(2)}) %collective-permute-start.10) | collective-permute-done | bytes 32800 | tf_op jit(solution)/shard_map/ppermute | solution.py:458
  62.7 3.7 %collective-permute-done.11.ret_next = bf16[128,128]{1,0:T(8,128)(2,1)S(1)} collective-permute-done((bf16[128,128]{1,0:T(8,128)(2,1)S(1)}, bf16[128,128]{1,0:T(8,128)(2,1)S(1)}, u32[]{:S(2)}, u32[]{:S(2)}) %collective-permute-start.11) | collective-permute-done | bytes 32800 | tf_op jit(solution)/shard_map/ppermute | solution.py:458
  66.3 4.7 %all-to-all-done.parts = bf16[32,56,128]{2,1,0:T(8,128)(2,1)S(1)} async-done(((bf16[32,56,128]{2,1,0:T(8,128)(2,1)}), bf16[32,56,128]{2,1,0:T(8,128)(2,1)S(1)}, u32[]{:S(2)}, u32[]{:S(2)}) %all-to-all-start) | async-done | bytes 458784 | tf_op jit(solution)/shard_map/all_to_all | solution.py:473
  71.0 0.1 sum_plane.1
  71.1 15.9 %all_to_all.15.parts = bf16[8,56,128]{2,1,0:T(8,128)(2,1)S(1)} all-to-all(bf16[8,56,128]{2,1,0:T(8,128)(2,1)S(1)} %sum_plane.1), channel_id=1, replica_groups=mesh['z'=8,'x'=4,'y'=4,'c'=2] {'z'}, dimensions={0} | all-to-all | bytes 229376 | tf_op jit(solution)/shard_map/all_to_all | solution.py:473
  87.0 0.8 sum_z.1
  87.8 4.8 %all-to-all-start.2 = ((bf16[32,56,128]{2,1,0:T(8,128)(2,1)}), bf16[32,56,128]{2,1,0:T(8,128)(2,1)S(1)}, u32[]{:S(2)}, u32[]{:S(2)}) async-start(bf16[32,56,128]{2,1,0:T(8,128)(2,1)} %sum_z.1), calls=%async_computation.2 | async-start | bytes 917504 | tf_op jit(solution)/shard_map/all_to_all | solution.py:473
  92.6 3.2 %fine_rest.1 = (bf16[3072,128]{1,0:T(8,128)(2,1)}, bf16[512,128]{1,0:T(8,128)(2,1)}) custom-call(s32[1,2]{1,0:T(1,128)S(1)} %copy-done.17, bf16[3072,128]{1,0:T(8,128)(2,1)S(1)} %get-tuple-element.110.grad_new, bf16[3072,128]{1,0:T(8,128)(2,1)S(1)} %get-tuple-element.111.ga, f32[512,128]{1,0:T(8,128)S(1)} %get-tuple-element.112.grad_part, ...), custom_call_target="tpu_custom_call" | custom-call | flops 1000000000 | bytes 2024456 | tf_op jit(solution)/shard_map/fine_rest/pallas_call | solution.py:42
  95.8 7.7 %all-to-all-done.2 = bf16[32,56,128]{2,1,0:T(8,128)(2,1)S(1)} async-done(((bf16[32,56,128]{2,1,0:T(8,128)(2,1)}), bf16[32,56,128]{2,1,0:T(8,128)(2,1)S(1)}, u32[]{:S(2)}, u32[]{:S(2)}) %all-to-all-start.2) | async-done | bytes 458784 | tf_op jit(solution)/shard_map/all_to_all | solution.py:473
  103.6 1.0 end.1
  (17 shorter events, 0.0 us)
Async XLA Ops:
  1.9 0.9 copy-start.3
  1.9 0.9 copy-start.16
  2.0 0.9 copy-start.17
  2.8 3.9 %copy-start = (bf16[3072,128]{1,0:T(8,128)(2,1)S(1)}, bf16[3072,128]{1,0:T(8,128)(2,1)}, u32[]{:S(2)}) copy-start(bf16[3072,128]{1,0:T(8,128)(2,1)} %edge.5) | copy-start | bytes 2359300
  2.8 3.9 %copy-start.4 = (bf16[512,128]{1,0:T(8,128)(2,1)S(1)}, bf16[512,128]{1,0:T(8,128)(2,1)}, u32[]{:S(2)}) copy-start(bf16[512,128]{1,0:T(8,128)(2,1)} %cot.3) | copy-start | bytes 393220
  2.9 3.9 %copy-start.5 = (bf16[384,128]{1,0:T(8,128)(2,1)S(1)}, bf16[384,128]{1,0:T(8,128)(2,1)}, u32[]{:S(2)}) copy-start(bf16[384,128]{1,0:T(8,128)(2,1)} %w_in.13) | copy-start | bytes 294916
  2.9 3.9 %copy-start.7 = (s32[3072]{0:T(1024)S(1)}, s32[3072]{0:T(1024)}, u32[]{:S(2)}) copy-start(s32[3072]{0:T(1024)} %param.22) | copy-start | bytes 36868
  2.9 3.9 %copy-start.8 = (s32[3072]{0:T(1024)S(1)}, s32[3072]{0:T(1024)}, u32[]{:S(2)}) copy-start(s32[3072]{0:T(1024)} %param.23) | copy-start | bytes 36868
  2.9 3.9 %copy-start.10 = (s32[512]{0:T(512)S(1)}, s32[512]{0:T(512)}, u32[]{:S(2)}) copy-start(s32[512]{0:T(512)} %param.27) | copy-start | bytes 6148
  3.3 5.8 %collective-permute-start = (bf16[128,128]{1,0:T(8,128)(2,1)S(1)}, bf16[128,128]{1,0:T(8,128)(2,1)S(1)}, u32[]{:S(2)}, u32[]{:S(2)}) collective-permute-start(bf16[128,128]{1,0:T(8,128)(2,1)S(1)} %get-tuple-element.67), channel_id=1, source_target_pairs={{0,1},{1,2},{2,3},{3,4},{4,5},{5,6},{6,7},{7,8},{8,9},{9,10},{10,1... | collective-permute-start | bytes 98312 | tf_op jit(solution)/shard_map/ppermute | solution.py:458
  6.1 3.3 %collective-permute-start.1 = (bf16[128,128]{1,0:T(8,128)(2,1)S(1)}, bf16[128,128]{1,0:T(8,128)(2,1)S(1)}, u32[]{:S(2)}, u32[]{:S(2)}) collective-permute-start(bf16[128,128]{1,0:T(8,128)(2,1)S(1)} %get-tuple-element.68), channel_id=1, source_target_pairs={{0,255},{1,0},{2,1},{3,2},{4,3},{5,4},{6,5},{7,6},{8,7},{9,8},{10,... | collective-permute-start | bytes 98312 | tf_op jit(solution)/shard_map/ppermute | solution.py:458
  6.8 2.7 %copy-start.2 = (bf16[5,128,128]{2,1,0:T(8,128)(2,1)S(1)}, bf16[5,128,128]{2,1,0:T(8,128)(2,1)}, u32[]{:S(2)}) copy-start(bf16[5,128,128]{2,1,0:T(8,128)(2,1)} %w_outs.11) | copy-start | bytes 491524
  6.8 2.7 %copy-start.6 = (bf16[256,128]{1,0:T(8,128)(2,1)S(1)}, bf16[256,128]{1,0:T(8,128)(2,1)}, u32[]{:S(2)}) copy-start(bf16[256,128]{1,0:T(8,128)(2,1)} %w_node.7) | copy-start | bytes 196612
  13.4 9.0 %collective-permute-start.2 = (bf16[528,128]{1,0:T(8,128)(2,1)S(1)}, bf16[528,128]{1,0:T(8,128)(2,1)S(1)}, u32[]{:S(2)}, u32[]{:S(2)}) collective-permute-start(bf16[528,128]{1,0:T(8,128)(2,1)S(1)} %get-tuple-element.70.a), channel_id=1, source_target_pairs={{0,1},{1,0},{2,3},{3,2},{4,5},{5,4},{6,7},{7,6},{8,9},{9,8},{10,11... | collective-permute-start | bytes 405512 | tf_op jit(solution)/shard_map/ppermute | solution.py:458
  22.4 4.9 %collective-permute-start.3 = (bf16[528,128]{1,0:T(8,128)(2,1)S(1)}, bf16[528,128]{1,0:T(8,128)(2,1)S(1)}, u32[]{:S(2)}, u32[]{:S(2)}) collective-permute-start(bf16[528,128]{1,0:T(8,128)(2,1)S(1)} %get-tuple-element.71.own), channel_id=1, source_target_pairs={{0,2},{1,7},{2,4},{3,1},{4,6},{5,3},{6,0},{7,5},{8,10},{9,15},{10,... | collective-permute-start | bytes 405512 | tf_op jit(solution)/shard_map/ppermute | solution.py:469
  22.5 4.8 %collective-permute-start.4 = (bf16[272,128]{1,0:T(8,128)(2,1)S(1)}, bf16[272,128]{1,0:T(8,128)(2,1)S(1)}, u32[]{:S(2)}, u32[]{:S(2)}) collective-permute-start(bf16[272,128]{1,0:T(8,128)(2,1)S(1)} %get-tuple-element.72), channel_id=1, source_target_pairs={{0,4},{2,6},{4,0},{6,2},{1,5},{3,7},{5,1},{7,3},{8,12},{10,14},{12... | collective-permute-start | bytes 208904 | tf_op jit(solution)/shard_map/ppermute | solution.py:458
  22.6 8.9 %copy-start.9 = (s32[1,2,128]{2,1,0:T(2,128)S(1)}, s32[1,2,128]{2,1,0:T(2,128)}, u32[]{:S(2)}) copy-start(s32[1,2,128]{2,1,0:T(2,128)} %param.31) | copy-start | bytes 3076
  22.6 8.9 %copy-start.11 = (s32[1,2]{1,0:T(1,128)S(1)}, s32[1,2]{1,0:T(1,128)}, u32[]{:S(2)}) copy-start(s32[1,2]{1,0:T(1,128)} %counts.6) | copy-start | bytes 28
  22.7 14.8 %copy-start.12 = (bf16[256,128]{1,0:T(8,128)(2,1)S(1)}, bf16[256,128]{1,0:T(8,128)(2,1)}, u32[]{:S(2)}) copy-start(bf16[256,128]{1,0:T(8,128)(2,1)} %w_node.6) | copy-start | bytes 196612
  22.7 14.8 %copy-start.13 = (bf16[256,128]{1,0:T(8,128)(2,1)S(1)}, bf16[256,128]{1,0:T(8,128)(2,1)}, u32[]{:S(2)}) copy-start(bf16[256,128]{1,0:T(8,128)(2,1)} %w_in.11) | copy-start | bytes 196612
  22.7 14.8 %copy-start.14 = (s32[1536]{0:T(1024)S(1)}, s32[1536]{0:T(1024)}, u32[]{:S(2)}) copy-start(s32[1536]{0:T(1024)} %param.28) | copy-start | bytes 18436
  22.7 14.8 %copy-start.15 = (s32[1536]{0:T(1024)S(1)}, s32[1536]{0:T(1024)}, u32[]{:S(2)}) copy-start(s32[1536]{0:T(1024)} %param.29) | copy-start | bytes 18436
  27.4 4.1 %collective-permute-start.5 = (bf16[528,128]{1,0:T(8,128)(2,1)S(1)}, bf16[528,128]{1,0:T(8,128)(2,1)S(1)}, u32[]{:S(2)}, u32[]{:S(2)}) collective-permute-start(bf16[528,128]{1,0:T(8,128)(2,1)S(1)} %join.1.a), channel_id=1, source_target_pairs={{0,1},{1,0},{2,3},{3,2},{4,5},{5,4},{6,7},{7,6},{8,9},{9,8},{10,11... | collective-permute-start | bytes 405512 | tf_op jit(solution)/shard_map/ppermute | solution.py:458
  32.0 6.7 %collective-permute-start.6 = (bf16[128,128]{1,0:T(8,128)(2,1)S(1)}, bf16[128,128]{1,0:T(8,128)(2,1)S(1)}, u32[]{:S(2)}, u32[]{:S(2)}) collective-permute-start(bf16[128,128]{1,0:T(8,128)(2,1)S(1)} %get-tuple-element.79), channel_id=1, source_target_pairs={{0,8},{8,16},{16,24},{24,32},{32,40},{40,48},{48,56},{56,64},{64,7... | collective-permute-start | bytes 98312 | tf_op jit(solution)/shard_map/ppermute | solution.py:458
  32.1 6.6 %collective-permute-start.7 = (bf16[128,128]{1,0:T(8,128)(2,1)S(1)}, bf16[128,128]{1,0:T(8,128)(2,1)S(1)}, u32[]{:S(2)}, u32[]{:S(2)}) collective-permute-start(bf16[128,128]{1,0:T(8,128)(2,1)S(1)} %get-tuple-element.80), channel_id=1, source_target_pairs={{0,248},{8,0},{16,8},{24,16},{32,24},{40,32},{48,40},{56,48},{64,5... | collective-permute-start | bytes 98312 | tf_op jit(solution)/shard_map/ppermute | solution.py:458
  42.4 6.6 %collective-permute-start.8 = (bf16[128,128]{1,0:T(8,128)(2,1)S(1)}, bf16[128,128]{1,0:T(8,128)(2,1)S(1)}, u32[]{:S(2)}, u32[]{:S(2)}) collective-permute-start(bf16[128,128]{1,0:T(8,128)(2,1)S(1)} %get-tuple-element.97), channel_id=1, source_target_pairs={{0,8},{8,16},{16,24},{24,32},{32,40},{40,48},{48,56},{56,64},{64,7... | collective-permute-start | bytes 98312 | tf_op jit(solution)/shard_map/ppermute | solution.py:458
  42.5 6.5 %collective-permute-start.9 = (bf16[128,128]{1,0:T(8,128)(2,1)S(1)}, bf16[128,128]{1,0:T(8,128)(2,1)S(1)}, u32[]{:S(2)}, u32[]{:S(2)}) collective-permute-start(bf16[128,128]{1,0:T(8,128)(2,1)S(1)} %get-tuple-element.98), channel_id=1, source_target_pairs={{0,248},{8,0},{16,8},{24,16},{32,24},{40,32},{48,40},{56,48},{64,5... | collective-permute-start | bytes 98312 | tf_op jit(solution)/shard_map/ppermute | solution.py:458
  47.7 1.3 %copy-start.1 = (bf16[3072,128]{1,0:T(8,128)(2,1)S(1)}, bf16[3072,128]{1,0:T(8,128)(2,1)}, u32[]{:S(2)}) copy-start(bf16[3072,128]{1,0:T(8,128)(2,1)} %cot_edges.1) | copy-start | bytes 2359300
  54.2 16.8 %all-to-all-start = ((bf16[32,56,128]{2,1,0:T(8,128)(2,1)}), bf16[32,56,128]{2,1,0:T(8,128)(2,1)S(1)}, u32[]{:S(2)}, u32[]{:S(2)}) async-start(bf16[32,56,128]{2,1,0:T(8,128)(2,1)} %bitcast.7), calls=%async_computation | async-start | bytes 917504 | tf_op jit(solution)/shard_map/all_to_all | solution.py:473
  59.8 2.9 %collective-permute-start.10 = (bf16[128,128]{1,0:T(8,128)(2,1)S(1)}, bf16[128,128]{1,0:T(8,128)(2,1)S(1)}, u32[]{:S(2)}, u32[]{:S(2)}) collective-permute-start(bf16[128,128]{1,0:T(8,128)(2,1)S(1)} %get-tuple-element.113), channel_id=1, source_target_pairs={{0,1},{1,2},{2,3},{3,4},{4,5},{5,6},{6,7},{7,8},{8,9},{9,10},{10,1... | collective-permute-start | bytes 98312 | tf_op jit(solution)/shard_map/ppermute | solution.py:458
  61.5 4.8 %collective-permute-start.11 = (bf16[128,128]{1,0:T(8,128)(2,1)S(1)}, bf16[128,128]{1,0:T(8,128)(2,1)S(1)}, u32[]{:S(2)}, u32[]{:S(2)}) collective-permute-start(bf16[128,128]{1,0:T(8,128)(2,1)S(1)} %get-tuple-element.114), channel_id=1, source_target_pairs={{0,255},{1,0},{2,1},{3,2},{4,3},{5,4},{6,5},{7,6},{8,7},{9,8},{10,... | collective-permute-start | bytes 98312 | tf_op jit(solution)/shard_map/ppermute | solution.py:458
  87.8 15.7 %all-to-all-start.2 = ((bf16[32,56,128]{2,1,0:T(8,128)(2,1)}), bf16[32,56,128]{2,1,0:T(8,128)(2,1)S(1)}, u32[]{:S(2)}, u32[]{:S(2)}) async-start(bf16[32,56,128]{2,1,0:T(8,128)(2,1)} %sum_z.1), calls=%async_computation.2 | async-start | bytes 917504 | tf_op jit(solution)/shard_map/all_to_all | solution.py:473
where the time goes:
time: 105 us
  starting transfers between devices  37.5 us (36%)
  Pallas kernels  25.5 us (24%)
  waiting for transfers between devices  22.4 us (21%)
  blocking collectives  15.9 us (15%)
  between operations  2.22 us (2%)
    ppermute x11, starting transfers between devices, shift(): lax.ppermute(value, axes, [(i, (i + step) % count) for i in range(count)])  27.1 us
    pallas_call x16, Pallas kernels, call(): pl.pallas_call(kernel, name=name, out_shape=out_shape, in_specs=[space] *...  25.5 us
    all_to_all x1, blocking collectives, exchange(): return lax.all_to_all(value, axes, 0, 0)  15.9 us
    all_to_all x2, waiting for transfers between devices, exchange(): return lax.all_to_all(value, axes, 0, 0)  12.4 us
    all_to_all x2, starting transfers between devices, exchange(): return lax.all_to_all(value, axes, 0, 0)  10.3 us
    ppermute x11, waiting for transfers between devices, shift(): lax.ppermute(value, axes, [(i, (i + step) % count) for i in range(count)])  10 us
  transfers between devices with their start and end apart: 14, of which 9 were waited for; matrix products, arithmetic and copies ran while one was open for 0% of the time, Pallas kernels for 9%

commit v1 on v0

--- a/solution.py
+++ b/solution.py
@@ -292,27 +292,31 @@
     pair_edge[0] = hidden
     pair_edge[1] = go
     ga = (dot_nt(go, w_outs[2]) * slope).astype(BF)
-    src_sums = dot(put(src_rows, blocks, NC + 2 * SLOT), ga).astype(BF)
+    src_sums = dot(put(src_rows - NC, blocks, 2 * SLOT), ga).astype(BF)
     sums_out[...] = src_sums
     ga_edge[...] = ga
     grad_ext = dot_nt(src_sums, w_in[:128, :])
-    back_prev[...] = grad_ext[NC : NC + SLOT].astype(BF)
-    back_next[...] = grad_ext[NC + SLOT :].astype(BF)
-    grad_own[...] = grad_total + grad_ext[:NC]
+    back_prev[...] = grad_ext[:SLOT].astype(BF)
+    back_next[...] = grad_ext[SLOT:].astype(BF)
+    grad_own[...] = grad_total
 
 
 def lift_kernel(
     own, cot, from_prev, from_next, coarse, grad_part, sums, agg, ga, pair_node, pair_edge,
-    ga_edge, dst, w_in, refined, pool, w_outs, new_nodes, grads, grad_own,
+    ga_edge, src, dst, w_in, refined, pool, w_outs, new_nodes, grads, grad_own,
 ):
     part = 1.0 / 8.0
     rows = own[...]
     ext = jnp.concatenate([rows, from_prev[...], from_next[...]], 0)
     dst_sums = dot(put(dst[...], range(EC // 128), NC), ga_edge[...]).astype(BF)
-    grad_own[...] = grad_part[...] + dot_nt(dst_sums, w_in[128:, :])
+    src_sums = dot(put(src[...], range(EC // 128), NC), ga_edge[...]).astype(BF)
+    grad_own[...] = (
+        grad_part[...] + dot_nt(src_sums, w_in[:128, :]) + dot_nt(dst_sums, w_in[128:, :])
+    )
+    src_sums = jnp.concatenate([src_sums, sums[...]], 0)
     lifted = dot(pick(columns(pool[...]), range(NF // 128), NC), coarse[...]).astype(BF)
     new_nodes[...] = (refined[...].astype(F32) + dot(lifted, w_outs[4])).astype(BF)
-    grads[0:128, :] = (part * dot_tn(ext, sums[...])).astype(BF)
+    grads[0:128, :] = (part * dot_tn(ext, src_sums)).astype(BF)
     grads[128:256, :] = (part * dot_tn(rows, dst_sums)).astype(BF)
     grads[256:384, :] = (part * dot_tn(rows, ga[...])).astype(BF)
     grads[384:512, :] = (part * dot_tn(agg[...], ga[...])).astype(BF)
@@ -348,8 +352,8 @@
 def fine_back_kernel(
     lives, counts, grad_own, divisor, ret_prev, ret_next, send, cot, pool, node, agg, src_rows,
     hidden, slope, normed, inv, hidden_node, slope_node, normed_node, inv_node, dst_rows, edge,
-    cot_edges, src, dst, w_in, w_node, w_outs, coarse_grads, grad_new, ga_out, grad_node, grads,
-    back_prev, back_next,
+    cot_edges, src, dst, w_in, w_node, w_outs, coarse_grads, grad_new, ga_out, grad_node, ga_node,
+    grads, back_prev, back_next,
 ):
     back = jnp.concatenate([ret_prev[...], ret_next[...]], 0)
     hot = put(live_slots(send[...], counts, GROUP), (0, 1), NC)
@@ -362,7 +366,8 @@
     grads[384:512, :] = dot_tn(node[...], ga).astype(BF)
     grads[512:640, :] = dot_tn(agg[...], ga).astype(BF)
     grads[1280:1408, :] = dot_tn(hidden_node[...], go).astype(BF)
-    grad_node[...] = grad_refined + dot_nt(ga, w_node[:128, :])
+    grad_node[...] = grad_refined.astype(BF)
+    ga_node[...] = ga
     dst_cols = columns(live_rows(dst[...], lives[0:1, 0:1]))
     slot_rows = src[...] - NF
     sums = jnp.zeros((2 * SLOT, L), F32)
@@ -395,7 +400,8 @@
 
 
 def fine_rest_kernel(
-    counts, grad_new, ga, grad_part, src, dst, w_in, ret_prev, ret_next, send, grad_edges_hbm,
+    counts, grad_new, ga, grad_part, ga_node, src, dst, w_in, w_node, ret_prev, ret_next, send,
+    grad_edges_hbm,
     grad_nodes, grad_edges, sems,
 ):
     src_rows, dst_rows = src[...], dst[...]
@@ -416,7 +422,8 @@
     back = jnp.concatenate([ret_prev[...], ret_next[...]], 0)
     hot = put(live_slots(send[...], counts, EVERY), (0, 1), NF)
     grad_nodes[...] = (
-        grad_part[...]
+        grad_part[...].astype(F32)
+        + dot_nt(ga_node[...], w_node[:128, :])
         + dot_nt(src_sums.astype(BF), w_in[128:256, :])
         + dot_nt(dst_sums.astype(BF), w_in[256:, :])
         + dot(hot, back)
@@ -527,7 +534,7 @@
     coarse, grad_part, back_prev, back_next, sums, cagg, cga, pair_node, pair_edge, cga_edge = call(
         coarse_kernel, "coarse",
         (shape(NC, L), f32(NC, L)) + slots
-        + (shape(NC + 2 * SLOT, L), shape(NC, L), shape(NC, L), shape(2, NC, L),
+        + (shape(2 * SLOT, L), shape(NC, L), shape(NC, L), shape(2, NC, L),
            shape(2, EC, L), shape(EC, L)),
         (lives, own, cpre, cpre_node, grad_coarse, cfrom_prev, cfrom_next, csrc, cdst,
          w_cedge, w_cnode, w_outs),
@@ -536,11 +543,11 @@
     new_nodes, coarse_grads, grad_own = call(
         lift_kernel, "lift", (shape(NF, L), shape(896, L), f32(NC, L)),
         (own, pooled_cot, cfrom_prev, cfrom_next, coarse, grad_part, sums, cagg, cga, pair_node,
-         pair_edge, cga_edge, cdst, w_cedge, refined, pool, w_outs),
-    )
-    grad_new, ga, grad_part, grads, back_prev, back_next = call(
+         pair_edge, cga_edge, csrc, cdst, w_cedge, refined, pool, w_outs),
+    )
+    grad_new, ga, grad_part, ga_node, grads, back_prev, back_next = call(
         fine_back_kernel, "fine_back",
-        (shape(EF, L), shape(EF, L), f32(NF, L), shape(GRADS, L)) + slots,
+        (shape(EF, L), shape(EF, L), shape(NF, L), shape(NF, L), shape(GRADS, L)) + slots,
         (lives, ccounts, grad_own, divisor, cret_prev, cret_next, csend, cot, pool, node, agg)
         + tuple(prepared)
         + (dst_rows, edge, cot_edges, src, dst, w_edge, w_node, w_outs, coarse_grads),
@@ -552,7 +559,8 @@
     )
     grad_edges, grad_nodes = call(
         fine_rest_kernel, "fine_rest", (shape(EF, L), shape(NF, L)),
-        (counts, grad_new, ga, grad_part, src, dst, w_edge, ret_prev, ret_next, send),
+        (counts, grad_new, ga, grad_part, ga_node, src, dst, w_edge, w_node, ret_prev, ret_next,
+         send),
         hbm_out=(0,), scratch=edge_copies,
     )
     parts = exchange(spread, "z")

time: 105 us -> 104 us (level)
  transfers between devices with their start and end apart: 14 -> 14, of which waited for: 9 -> 9; matrix products, arithmetic and copies ran while one was open for 0% -> 0% of each run, Pallas kernels for 9% -> 10%
where the time goes in v1:
time: 104 us
  starting transfers between devices  37.3 us (36%)
  Pallas kernels  25.3 us (24%)
  waiting for transfers between devices  22.4 us (22%)
  blocking collectives  15.9 us (15%)
  between operations  2.22 us (2%)
    ppermute x11, starting transfers between devices, shift(): lax.ppermute(value, axes, [(i, (i + step) % count) for i in range(count)])  27.1 us
    pallas_call x16, Pallas kernels, call(): pl.pallas_call(kernel, name=name, out_shape=out_shape, in_specs=[space] *...  25.3 us
    all_to_all x1, blocking collectives, exchange(): return lax.all_to_all(value, axes, 0, 0)  15.9 us
    all_to_all x2, waiting for transfers between devices, exchange(): return lax.all_to_all(value, axes, 0, 0)  12.3 us
    all_to_all x2, starting transfers between devices, exchange(): return lax.all_to_all(value, axes, 0, 0)  10.1 us
    ppermute x11, waiting for transfers between devices, shift(): lax.ppermute(value, axes, [(i, (i + step) % count) for i in range(count)])  10 us
  transfers between devices with their start and end apart: 14, of which 9 were waited for; matrix products, arithmetic and copies ran while one was open for 0% of the time, Pallas kernels for 10%

profile of v1, /device:TPU:1, one launch (start us, length us, event | category | flops | bytes accessed | tf_op | source)
XLA Modules:
  0.0 104.1 jit_solution(3584869894512788782)
XLA Ops:
  1.9 0.0 copy-start.3
  1.9 0.0 copy-start.16
  2.0 0.0 copy-start.17
  2.0 0.9 copy-done.3
  2.8 0.0 copy-done.16
  2.9 0.0 copy-start.5
  2.9 0.0 copy-start.7
  2.9 0.0 copy-start.8
  2.9 0.0 copy-start.10
  2.9 0.4 send.1
  3.3 2.8 %collective-permute-start = (bf16[128,128]{1,0:T(8,128)(2,1)S(1)}, bf16[128,128]{1,0:T(8,128)(2,1)S(1)}, u32[]{:S(2)}, u32[]{:S(2)}) collective-permute-start(bf16[128,128]{1,0:T(8,128)(2,1)S(1)} %get-tuple-element.68), channel_id=1, source_target_pairs={{0,1},{1,2},{2,3},{3,4},{4,5},{5,6},{6,7},{7,8},{8,9},{9,10},{10,1... | collective-permute-start | bytes 98312 | tf_op jit(solution)/shard_map/ppermute | solution.py:465
  6.1 0.6 collective-permute-start.1
  6.7 0.0 copy-done.4
  6.8 0.0 copy-start.2
  6.8 0.0 copy-start.6
  6.8 2.3 %pre.1 = (f32[3072,128]{1,0:T(8,128)S(1)}, bf16[272,128]{1,0:T(8,128)(2,1)S(1)}, bf16[3072,128]{1,0:T(8,128)(2,1)S(1)}, bf16[3072,128]{1,0:T(8,128)(2,1)S(1)}) custom-call(bf16[512,128]{1,0:T(8,128)(2,1)S(1)} %copy-done.3, bf16[384,128]{1,0:T(8,128)(2,1)S(1)} %copy-done.5, s32[24,128]{1,0:T(8,128)S(1)} %bitcast.10, s32[24,128]{1,0:T(8,128)S(1)} %bitcast.15, ...), custom_call_target="tpu_custom_call" | custom-call | flops 1000000000 | bytes 1173504 | tf_op jit(solution)/shard_map/pre/pallas_call | solution.py:42
  9.1 0.0 collective-permute-done.from_prev
  9.1 0.3 collective-permute-done.1.from_next
  9.4 3.9 %fine.1 = (bf16[3072,128]{1,0:T(8,128)(2,1)}, f32[3072,128]{1,0:T(8,128)S(1)}, bf16[512,128]{1,0:T(8,128)(2,1)S(1)}, f32[512,128]{1,0:T(8,128)S(1)}, bf16[512,12...) custom-call(s32[8,128]{1,0:T(8,128)S(1)} %begin.1.lives.live, f32[3072,128]{1,0:T(8,128)S(1)} %get-tuple-element.67.pre, ...), custom_call_target="tpu_custom_call" | custom-call | flops 1000000000 | bytes 2983936 | tf_op jit(solution)/shard_map/fine/pallas_call | solution.py:42
  13.4 8.0 %collective-permute-start.2 = (bf16[528,128]{1,0:T(8,128)(2,1)S(1)}, bf16[528,128]{1,0:T(8,128)(2,1)S(1)}, u32[]{:S(2)}, u32[]{:S(2)}) collective-permute-start(bf16[528,128]{1,0:T(8,128)(2,1)S(1)} %get-tuple-element.71.a), channel_id=1, source_target_pairs={{0,1},{1,0},{2,3},{3,2},{4,5},{5,4},{6,7},{7,6},{8,9},{9,8},{10,11... | collective-permute-start | bytes 405512 | tf_op jit(solution)/shard_map/ppermute | solution.py:465
  21.4 1.0 collective-permute-done.2.b
  22.4 0.1 pair.1
  22.4 0.1 collective-permute-start.3
  22.5 0.1 collective-permute-start.4
  22.6 0.0 copy-start.9
  22.6 0.0 copy-start.11
  22.7 0.0 copy-start.12
  22.7 0.0 copy-start.13
  22.7 0.0 copy-start.14
  22.7 0.0 copy-start.15
  22.7 2.0 %prep.1 = (bf16[3072,128]{1,0:T(8,128)(2,1)S(1)}, bf16[3072,128]{1,0:T(8,128)(2,1)S(1)}, bf16[3072,128]{1,0:T(8,128)(2,1)S(1)}, bf16[3072,128]{1,0:T(8,128)(2,1)...) custom-call(f32[3072,128]{1,0:T(8,128)S(1)} %get-tuple-element.74.ac, ...), custom_call_target="tpu_custom_call" | custom-call | flops 1000000000 | bytes 2863104 | tf_op jit(solution)/shard_map/prep/pallas_call | solution.py:42
  24.7 2.6 %collective-permute-done.4.part = bf16[272,128]{1,0:T(8,128)(2,1)S(1)} collective-permute-done((bf16[272,128]{1,0:T(8,128)(2,1)S(1)}, bf16[272,128]{1,0:T(8,128)(2,1)S(1)}, u32[]{:S(2)}, u32[]{:S(2)}) %collective-permute-start.4) | collective-permute-done | bytes 69664 | tf_op jit(solution)/shard_map/ppermute | solution.py:465
  27.3 0.0 collective-permute-done.3.near
  27.3 0.1 join.1.a
  27.4 3.1 %collective-permute-start.5 = (bf16[528,128]{1,0:T(8,128)(2,1)S(1)}, bf16[528,128]{1,0:T(8,128)(2,1)S(1)}, u32[]{:S(2)}, u32[]{:S(2)}) collective-permute-start(bf16[528,128]{1,0:T(8,128)(2,1)S(1)} %join.1.a), channel_id=1, source_target_pairs={{0,1},{1,0},{2,3},{3,2},{4,5},{5,4},{6,7},{7,6},{8,9},{9,8},{10,11... | collective-permute-start | bytes 405512 | tf_op jit(solution)/shard_map/ppermute | solution.py:465
  30.5 1.0 collective-permute-done.5.b
  31.5 0.4 pool.1
  32.0 0.1 collective-permute-start.6
  32.1 5.4 %collective-permute-start.7 = (bf16[128,128]{1,0:T(8,128)(2,1)S(1)}, bf16[128,128]{1,0:T(8,128)(2,1)S(1)}, u32[]{:S(2)}, u32[]{:S(2)}) collective-permute-start(bf16[128,128]{1,0:T(8,128)(2,1)S(1)} %get-tuple-element.81), channel_id=1, source_target_pairs={{0,248},{8,0},{16,8},{24,16},{32,24},{40,32},{48,40},{56,48},{64,5... | collective-permute-start | bytes 98312 | tf_op jit(solution)/shard_map/ppermute | solution.py:465
  37.5 0.0 copy-done.13
  37.5 0.0 copy-done.15
  37.5 0.9 coarse_pre.1
  38.3 0.3 collective-permute-done.6.from_prev
  38.7 0.0 collective-permute-done.7.from_next
  38.7 3.1 %coarse.1 = (bf16[256,128]{1,0:T(8,128)(2,1)S(1)}, f32[256,128]{1,0:T(8,128)S(1)}, bf16[128,128]{1,0:T(8,128)(2,1)S(1)}, bf16[128,128]{1,0:T(8,128)(2,1)S(1)}, b...) custom-call(s32[8,128]{1,0:T(8,128)S(1)} %begin.1.lives.live, ...), custom_call_target="tpu_custom_call" | custom-call | flops 1000000000 | bytes 1425408 | tf_op jit(solution)/shard_map/coarse/pallas_call | solution.py:42
  41.8 0.1 collective-permute-start.8
  41.9 5.2 %collective-permute-start.9 = (bf16[128,128]{1,0:T(8,128)(2,1)S(1)}, bf16[128,128]{1,0:T(8,128)(2,1)S(1)}, u32[]{:S(2)}, u32[]{:S(2)}) collective-permute-start(bf16[128,128]{1,0:T(8,128)(2,1)S(1)} %get-tuple-element.99), channel_id=1, source_target_pairs={{0,248},{8,0},{16,8},{24,16},{32,24},{40,32},{48,40},{56,48},{64,5... | collective-permute-start | bytes 98312 | tf_op jit(solution)/shard_map/ppermute | solution.py:465
  47.0 1.5 %lift.1 = (bf16[512,128]{1,0:T(8,128)(2,1)}, bf16[896,128]{1,0:T(8,128)(2,1)S(1)}, f32[256,128]{1,0:T(8,128)S(1)}) custom-call(bf16[256,128]{1,0:T(8,128)(2,1)S(1)} %get-tuple-element.78.own, bf16[256,128]{1,0:T(8,128)(2,1)S(1)} %get-tuple-element.79.cot, bf16[128,128]{1,0:T(8,128)(2,1)S(1)} %collective-permute-done.6.from_prev, ...), custom_call_target="tpu_custom_call" | custom-call | flops 1000000000 | bytes 2275328 | tf_op jit(solution)/shard_map/lift/pallas_call | solution.py:42
  48.6 0.0 collective-permute-done.8.ret_prev
  48.6 0.0 collective-permute-done.9.ret_next
  48.6 5.4 %fine_back.1 = (bf16[3072,128]{1,0:T(8,128)(2,1)S(1)}, bf16[3072,128]{1,0:T(8,128)(2,1)S(1)}, bf16[512,128]{1,0:T(8,128)(2,1)S(1)}, bf16[512,128]{1,0:T(8,128)(2...) custom-call(s32[8,128]{1,0:T(8,128)S(1)} %begin.1.lives.live, ...), custom_call_target="tpu_custom_call" | custom-call | flops 1000000000 | bytes 7484424 | tf_op jit(solution)/shard_map/fine_back/pallas_call | solution.py:42
  54.0 5.3 %all-to-all-start = ((bf16[32,56,128]{2,1,0:T(8,128)(2,1)}), bf16[32,56,128]{2,1,0:T(8,128)(2,1)S(1)}, u32[]{:S(2)}, u32[]{:S(2)}) async-start(bf16[32,56,128]{2,1,0:T(8,128)(2,1)} %bitcast.7), calls=%async_computation | async-start | bytes 917504 | tf_op jit(solution)/shard_map/all_to_all | solution.py:480
  59.3 1.7 %collective-permute-start.10 = (bf16[128,128]{1,0:T(8,128)(2,1)S(1)}, bf16[128,128]{1,0:T(8,128)(2,1)S(1)}, u32[]{:S(2)}, u32[]{:S(2)}) collective-permute-start(bf16[128,128]{1,0:T(8,128)(2,1)S(1)} %get-tuple-element.115), channel_id=1, source_target_pairs={{0,1},{1,2},{2,3},{3,4},{4,5},{5,6},{6,7},{7,8},{8,9},{9,10},{10,1... | collective-permute-start | bytes 98312 | tf_op jit(solution)/shard_map/ppermute | solution.py:465
  61.0 0.0 collective-permute-start.11
  61.0 1.2 %collective-permute-done.10.ret_prev = bf16[128,128]{1,0:T(8,128)(2,1)S(1)} collective-permute-done((bf16[128,128]{1,0:T(8,128)(2,1)S(1)}, bf16[128,128]{1,0:T(8,128)(2,1)S(1)}, u32[]{:S(2)}, u32[]{:S(2)}) %collective-permute-start.10) | collective-permute-done | bytes 32800 | tf_op jit(solution)/shard_map/ppermute | solution.py:465
  62.2 3.7 %collective-permute-done.11.ret_next = bf16[128,128]{1,0:T(8,128)(2,1)S(1)} collective-permute-done((bf16[128,128]{1,0:T(8,128)(2,1)S(1)}, bf16[128,128]{1,0:T(8,128)(2,1)S(1)}, u32[]{:S(2)}, u32[]{:S(2)}) %collective-permute-start.11) | collective-permute-done | bytes 32800 | tf_op jit(solution)/shard_map/ppermute | solution.py:465
  65.9 4.7 %all-to-all-done.parts = bf16[32,56,128]{2,1,0:T(8,128)(2,1)S(1)} async-done(((bf16[32,56,128]{2,1,0:T(8,128)(2,1)}), bf16[32,56,128]{2,1,0:T(8,128)(2,1)S(1)}, u32[]{:S(2)}, u32[]{:S(2)}) %all-to-all-start) | async-done | bytes 458784 | tf_op jit(solution)/shard_map/all_to_all | solution.py:480
  70.5 0.1 sum_plane.1
  70.6 15.9 %all_to_all.15.parts = bf16[8,56,128]{2,1,0:T(8,128)(2,1)S(1)} all-to-all(bf16[8,56,128]{2,1,0:T(8,128)(2,1)S(1)} %sum_plane.1), channel_id=1, replica_groups=mesh['z'=8,'x'=4,'y'=4,'c'=2] {'z'}, dimensions={0} | all-to-all | bytes 229376 | tf_op jit(solution)/shard_map/all_to_all | solution.py:480
  86.6 0.8 sum_z.1
  87.4 4.8 %all-to-all-start.2 = ((bf16[32,56,128]{2,1,0:T(8,128)(2,1)}), bf16[32,56,128]{2,1,0:T(8,128)(2,1)S(1)}, u32[]{:S(2)}, u32[]{:S(2)}) async-start(bf16[32,56,128]{2,1,0:T(8,128)(2,1)} %sum_z.1), calls=%async_computation.2 | async-start | bytes 917504 | tf_op jit(solution)/shard_map/all_to_all | solution.py:480
  92.1 3.3 %fine_rest.1 = (bf16[3072,128]{1,0:T(8,128)(2,1)}, bf16[512,128]{1,0:T(8,128)(2,1)}) custom-call(s32[1,2]{1,0:T(1,128)S(1)} %copy-done.17, bf16[3072,128]{1,0:T(8,128)(2,1)S(1)} %get-tuple-element.111.grad_new, bf16[3072,128]{1,0:T(8,128)(2,1)S(1)} %get-tuple-element.112.ga, bf16[512,128]{1,0:T(8,128)(2,1)S(1)} %get-tuple-element.113.grad_part, ...), custom_call_target="tpu_custom_call" | custom-call | flops 1000000000 | bytes 2089992 | tf_op jit(solution)/shard_map/fine_rest/pallas_call | solution.py:42
  95.4 7.7 %all-to-all-done.2 = bf16[32,56,128]{2,1,0:T(8,128)(2,1)S(1)} async-done(((bf16[32,56,128]{2,1,0:T(8,128)(2,1)}), bf16[32,56,128]{2,1,0:T(8,128)(2,1)S(1)}, u32[]{:S(2)}, u32[]{:S(2)}) %all-to-all-start.2) | async-done | bytes 458784 | tf_op jit(solution)/shard_map/all_to_all | solution.py:480
  103.1 1.0 end.1
  (17 shorter events, 0.0 us)
Async XLA Ops:
  1.9 0.9 copy-start.3
  1.9 0.9 copy-start.16
  2.0 0.9 copy-start.17
  2.8 3.9 %copy-start = (bf16[3072,128]{1,0:T(8,128)(2,1)S(1)}, bf16[3072,128]{1,0:T(8,128)(2,1)}, u32[]{:S(2)}) copy-start(bf16[3072,128]{1,0:T(8,128)(2,1)} %edge.5) | copy-start | bytes 2359300
  2.8 3.9 %copy-start.4 = (bf16[512,128]{1,0:T(8,128)(2,1)S(1)}, bf16[512,128]{1,0:T(8,128)(2,1)}, u32[]{:S(2)}) copy-start(bf16[512,128]{1,0:T(8,128)(2,1)} %cot.3) | copy-start | bytes 393220
  2.9 3.9 %copy-start.5 = (bf16[384,128]{1,0:T(8,128)(2,1)S(1)}, bf16[384,128]{1,0:T(8,128)(2,1)}, u32[]{:S(2)}) copy-start(bf16[384,128]{1,0:T(8,128)(2,1)} %w_in.13) | copy-start | bytes 294916
  2.9 3.9 %copy-start.7 = (s32[3072]{0:T(1024)S(1)}, s32[3072]{0:T(1024)}, u32[]{:S(2)}) copy-start(s32[3072]{0:T(1024)} %param.22) | copy-start | bytes 36868
  2.9 3.9 %copy-start.8 = (s32[3072]{0:T(1024)S(1)}, s32[3072]{0:T(1024)}, u32[]{:S(2)}) copy-start(s32[3072]{0:T(1024)} %param.23) | copy-start | bytes 36868
  2.9 3.9 %copy-start.10 = (s32[512]{0:T(512)S(1)}, s32[512]{0:T(512)}, u32[]{:S(2)}) copy-start(s32[512]{0:T(512)} %param.27) | copy-start | bytes 6148
  3.3 5.8 %collective-permute-start = (bf16[128,128]{1,0:T(8,128)(2,1)S(1)}, bf16[128,128]{1,0:T(8,128)(2,1)S(1)}, u32[]{:S(2)}, u32[]{:S(2)}) collective-permute-start(bf16[128,128]{1,0:T(8,128)(2,1)S(1)} %get-tuple-element.68), channel_id=1, source_target_pairs={{0,1},{1,2},{2,3},{3,4},{4,5},{5,6},{6,7},{7,8},{8,9},{9,10},{10,1... | collective-permute-start | bytes 98312 | tf_op jit(solution)/shard_map/ppermute | solution.py:465
  6.1 3.3 %collective-permute-start.1 = (bf16[128,128]{1,0:T(8,128)(2,1)S(1)}, bf16[128,128]{1,0:T(8,128)(2,1)S(1)}, u32[]{:S(2)}, u32[]{:S(2)}) collective-permute-start(bf16[128,128]{1,0:T(8,128)(2,1)S(1)} %get-tuple-element.69), channel_id=1, source_target_pairs={{0,255},{1,0},{2,1},{3,2},{4,3},{5,4},{6,5},{7,6},{8,7},{9,8},{10,... | collective-permute-start | bytes 98312 | tf_op jit(solution)/shard_map/ppermute | solution.py:465
  6.8 2.7 %copy-start.2 = (bf16[5,128,128]{2,1,0:T(8,128)(2,1)S(1)}, bf16[5,128,128]{2,1,0:T(8,128)(2,1)}, u32[]{:S(2)}) copy-start(bf16[5,128,128]{2,1,0:T(8,128)(2,1)} %w_outs.11) | copy-start | bytes 491524
  6.8 2.7 %copy-start.6 = (bf16[256,128]{1,0:T(8,128)(2,1)S(1)}, bf16[256,128]{1,0:T(8,128)(2,1)}, u32[]{:S(2)}) copy-start(bf16[256,128]{1,0:T(8,128)(2,1)} %w_node.9) | copy-start | bytes 196612
  13.4 9.0 %collective-permute-start.2 = (bf16[528,128]{1,0:T(8,128)(2,1)S(1)}, bf16[528,128]{1,0:T(8,128)(2,1)S(1)}, u32[]{:S(2)}, u32[]{:S(2)}) collective-permute-start(bf16[528,128]{1,0:T(8,128)(2,1)S(1)} %get-tuple-element.71.a), channel_id=1, source_target_pairs={{0,1},{1,0},{2,3},{3,2},{4,5},{5,4},{6,7},{7,6},{8,9},{9,8},{10,11... | collective-permute-start | bytes 405512 | tf_op jit(solution)/shard_map/ppermute | solution.py:465
  22.4 4.9 %collective-permute-start.3 = (bf16[528,128]{1,0:T(8,128)(2,1)S(1)}, bf16[528,128]{1,0:T(8,128)(2,1)S(1)}, u32[]{:S(2)}, u32[]{:S(2)}) collective-permute-start(bf16[528,128]{1,0:T(8,128)(2,1)S(1)} %get-tuple-element.72.own), channel_id=1, source_target_pairs={{0,2},{1,7},{2,4},{3,1},{4,6},{5,3},{6,0},{7,5},{8,10},{9,15},{10,... | collective-permute-start | bytes 405512 | tf_op jit(solution)/shard_map/ppermute | solution.py:476
  22.5 4.8 %collective-permute-start.4 = (bf16[272,128]{1,0:T(8,128)(2,1)S(1)}, bf16[272,128]{1,0:T(8,128)(2,1)S(1)}, u32[]{:S(2)}, u32[]{:S(2)}) collective-permute-start(bf16[272,128]{1,0:T(8,128)(2,1)S(1)} %get-tuple-element.73), channel_id=1, source_target_pairs={{0,4},{2,6},{4,0},{6,2},{1,5},{3,7},{5,1},{7,3},{8,12},{10,14},{12... | collective-permute-start | bytes 208904 | tf_op jit(solution)/shard_map/ppermute | solution.py:465
  22.6 8.9 %copy-start.9 = (s32[1,2,128]{2,1,0:T(2,128)S(1)}, s32[1,2,128]{2,1,0:T(2,128)}, u32[]{:S(2)}) copy-start(s32[1,2,128]{2,1,0:T(2,128)} %param.31) | copy-start | bytes 3076
  22.6 8.9 %copy-start.11 = (s32[1,2]{1,0:T(1,128)S(1)}, s32[1,2]{1,0:T(1,128)}, u32[]{:S(2)}) copy-start(s32[1,2]{1,0:T(1,128)} %counts.6) | copy-start | bytes 28
  22.7 14.8 %copy-start.12 = (bf16[256,128]{1,0:T(8,128)(2,1)S(1)}, bf16[256,128]{1,0:T(8,128)(2,1)}, u32[]{:S(2)}) copy-start(bf16[256,128]{1,0:T(8,128)(2,1)} %w_node.7) | copy-start | bytes 196612
  22.7 14.8 %copy-start.13 = (bf16[256,128]{1,0:T(8,128)(2,1)S(1)}, bf16[256,128]{1,0:T(8,128)(2,1)}, u32[]{:S(2)}) copy-start(bf16[256,128]{1,0:T(8,128)(2,1)} %w_in.11) | copy-start | bytes 196612
  22.7 14.8 %copy-start.14 = (s32[1536]{0:T(1024)S(1)}, s32[1536]{0:T(1024)}, u32[]{:S(2)}) copy-start(s32[1536]{0:T(1024)} %param.28) | copy-start | bytes 18436
  22.7 14.8 %copy-start.15 = (s32[1536]{0:T(1024)S(1)}, s32[1536]{0:T(1024)}, u32[]{:S(2)}) copy-start(s32[1536]{0:T(1024)} %param.29) | copy-start | bytes 18436
  27.4 4.1 %collective-permute-start.5 = (bf16[528,128]{1,0:T(8,128)(2,1)S(1)}, bf16[528,128]{1,0:T(8,128)(2,1)S(1)}, u32[]{:S(2)}, u32[]{:S(2)}) collective-permute-start(bf16[528,128]{1,0:T(8,128)(2,1)S(1)} %join.1.a), channel_id=1, source_target_pairs={{0,1},{1,0},{2,3},{3,2},{4,5},{5,4},{6,7},{7,6},{8,9},{9,8},{10,11... | collective-permute-start | bytes 405512 | tf_op jit(solution)/shard_map/ppermute | solution.py:465
  32.0 6.7 %collective-permute-start.6 = (bf16[128,128]{1,0:T(8,128)(2,1)S(1)}, bf16[128,128]{1,0:T(8,128)(2,1)S(1)}, u32[]{:S(2)}, u32[]{:S(2)}) collective-permute-start(bf16[128,128]{1,0:T(8,128)(2,1)S(1)} %get-tuple-element.80), channel_id=1, source_target_pairs={{0,8},{8,16},{16,24},{24,32},{32,40},{40,48},{48,56},{56,64},{64,7... | collective-permute-start | bytes 98312 | tf_op jit(solution)/shard_map/ppermute | solution.py:465
  32.1 6.6 %collective-permute-start.7 = (bf16[128,128]{1,0:T(8,128)(2,1)S(1)}, bf16[128,128]{1,0:T(8,128)(2,1)S(1)}, u32[]{:S(2)}, u32[]{:S(2)}) collective-permute-start(bf16[128,128]{1,0:T(8,128)(2,1)S(1)} %get-tuple-element.81), channel_id=1, source_target_pairs={{0,248},{8,0},{16,8},{24,16},{32,24},{40,32},{48,40},{56,48},{64,5... | collective-permute-start | bytes 98312 | tf_op jit(solution)/shard_map/ppermute | solution.py:465
  41.8 6.8 %collective-permute-start.8 = (bf16[128,128]{1,0:T(8,128)(2,1)S(1)}, bf16[128,128]{1,0:T(8,128)(2,1)S(1)}, u32[]{:S(2)}, u32[]{:S(2)}) collective-permute-start(bf16[128,128]{1,0:T(8,128)(2,1)S(1)} %get-tuple-element.98), channel_id=1, source_target_pairs={{0,8},{8,16},{16,24},{24,32},{32,40},{40,48},{48,56},{56,64},{64,7... | collective-permute-start | bytes 98312 | tf_op jit(solution)/shard_map/ppermute | solution.py:465
  41.9 6.7 %collective-permute-start.9 = (bf16[128,128]{1,0:T(8,128)(2,1)S(1)}, bf16[128,128]{1,0:T(8,128)(2,1)S(1)}, u32[]{:S(2)}, u32[]{:S(2)}) collective-permute-start(bf16[128,128]{1,0:T(8,128)(2,1)S(1)} %get-tuple-element.99), channel_id=1, source_target_pairs={{0,248},{8,0},{16,8},{24,16},{32,24},{40,32},{48,40},{56,48},{64,5... | collective-permute-start | bytes 98312 | tf_op jit(solution)/shard_map/ppermute | solution.py:465
  47.0 1.5 %copy-start.1 = (bf16[3072,128]{1,0:T(8,128)(2,1)S(1)}, bf16[3072,128]{1,0:T(8,128)(2,1)}, u32[]{:S(2)}) copy-start(bf16[3072,128]{1,0:T(8,128)(2,1)} %cot_edges.1) | copy-start | bytes 2359300
  54.0 16.6 %all-to-all-start = ((bf16[32,56,128]{2,1,0:T(8,128)(2,1)}), bf16[32,56,128]{2,1,0:T(8,128)(2,1)S(1)}, u32[]{:S(2)}, u32[]{:S(2)}) async-start(bf16[32,56,128]{2,1,0:T(8,128)(2,1)} %bitcast.7), calls=%async_computation | async-start | bytes 917504 | tf_op jit(solution)/shard_map/all_to_all | solution.py:480
  59.3 2.9 %collective-permute-start.10 = (bf16[128,128]{1,0:T(8,128)(2,1)S(1)}, bf16[128,128]{1,0:T(8,128)(2,1)S(1)}, u32[]{:S(2)}, u32[]{:S(2)}) collective-permute-start(bf16[128,128]{1,0:T(8,128)(2,1)S(1)} %get-tuple-element.115), channel_id=1, source_target_pairs={{0,1},{1,2},{2,3},{3,4},{4,5},{5,6},{6,7},{7,8},{8,9},{9,10},{10,1... | collective-permute-start | bytes 98312 | tf_op jit(solution)/shard_map/ppermute | solution.py:465
  61.0 4.8 %collective-permute-start.11 = (bf16[128,128]{1,0:T(8,128)(2,1)S(1)}, bf16[128,128]{1,0:T(8,128)(2,1)S(1)}, u32[]{:S(2)}, u32[]{:S(2)}) collective-permute-start(bf16[128,128]{1,0:T(8,128)(2,1)S(1)} %get-tuple-element.116), channel_id=1, source_target_pairs={{0,255},{1,0},{2,1},{3,2},{4,3},{5,4},{6,5},{7,6},{8,7},{9,8},{10,... | collective-permute-start | bytes 98312 | tf_op jit(solution)/shard_map/ppermute | solution.py:465
  87.4 15.7 %all-to-all-start.2 = ((bf16[32,56,128]{2,1,0:T(8,128)(2,1)}), bf16[32,56,128]{2,1,0:T(8,128)(2,1)S(1)}, u32[]{:S(2)}, u32[]{:S(2)}) async-start(bf16[32,56,128]{2,1,0:T(8,128)(2,1)} %sum_z.1), calls=%async_computation.2 | async-start | bytes 917504 | tf_op jit(solution)/shard_map/all_to_all | solution.py:480

commit v2 on v1

--- a/solution.py
+++ b/solution.py
@@ -118,6 +118,24 @@
     )
 
 
+def even(axes):
+    return lax.rem(lax.axis_index(axes[-1]), 2) == 0
+
+
+def to_mates(prev, following, axes):
+    here = even(axes)
+    return (
+        jnp.where(here, following, prev).astype(BF), jnp.where(here, prev, following).astype(BF)
+    )
+
+
+def by_side(first, second, axes):
+    first, second, here = first[...].astype(F32), second[...].astype(F32), even(axes)
+    return jnp.concatenate(
+        [jnp.where(here, second, first), jnp.where(here, first, second)], 0
+    ).astype(BF)
+
+
 def sigmoid(a):
     return 1.0 / (1.0 + jnp.exp(-a))
 
@@ -147,11 +165,11 @@
     out[...] = jnp.where(at == 0, live[0], jnp.where(at == 1, clive[0], 0))
 
 
-def send_kernel(lives, node, send, counts, to_prev, to_next):
+def send_kernel(lives, node, send, counts, first, second):
     cols = columns(live_slots(send[...] + lives[2:4, :], counts, EVERY))
     rows = node[...]
-    to_prev[...] = dot(pick(cols, (0,), NF), rows).astype(BF)
-    to_next[...] = dot(pick(cols, (1,), NF), rows).astype(BF)
+    to_prev, to_next = dot(pick(cols, (0,), NF), rows), dot(pick(cols, (1,), NF), rows)
+    first[...], second[...] = to_mates(to_prev, to_next, EVERY)
 
 
 def pre_kernel(node, w_in, src, dst, edge, pool, cot, pre, side, src_rows, dst_rows):
@@ -181,10 +199,10 @@
 
 
 def fine_kernel(
-    live, pre, edge, node, from_prev, from_next, src, dst, w_in, w_node, w_outs, pool, side,
+    live, pre, edge, node, from_first, from_second, src, dst, w_in, w_node, w_outs, pool, side,
     new_edges_hbm, act, agg_out, act_node, refined, payload, new_edges, sems,
 ):
-    halo = jnp.concatenate([from_prev[...], from_next[...]], 0)
+    halo = by_side(from_first, from_second, EVERY)
     table = dot(halo, w_in[128:256, :]).astype(BF)
     src_cols = columns(src[...] - NF)
     dst_rows = live_rows(dst[...], live[0:1, 0:1])
@@ -231,7 +249,7 @@
     out[...] = total[...].astype(BF)
 
 
-def pool_kernel(a, b, send, counts, own_out, cot_out, divisor, to_prev, to_next):
+def pool_kernel(a, b, send, counts, own_out, cot_out, divisor, first, second):
     total = a[...].astype(F32) + b[...].astype(F32)
     lines = total[2 * NC :, :]
     count = 16.0 * lines[0:2, :] + lines[2:4, :]
@@ -244,8 +262,8 @@
     cot_out[...] = total[NC : 2 * NC, :].astype(BF)
     divisor[...] = count
     cols = columns(live_slots(send[...], counts, GROUP))
-    to_prev[...] = dot(pick(cols, (0,), NC), own).astype(BF)
-    to_next[...] = dot(pick(cols, (1,), NC), own).astype(BF)
+    to_prev, to_next = dot(pick(cols, (0,), NC), own), dot(pick(cols, (1,), NC), own)
+    first[...], second[...] = to_mates(to_prev, to_next, GROUP)
 
 
 def coarse_pre_kernel(own, cot, src, dst, w_in, w_node, w_outs, pre, pre_node, grad_coarse):
@@ -261,10 +279,10 @@
 
 
 def coarse_kernel(
-    live, own, pre, pre_node, grad_coarse, from_prev, from_next, src, dst, w_in, w_node, w_outs,
-    coarse_out, grad_own, back_prev, back_next, sums_out, agg_out, ga_out, pair_node, pair_edge, ga_edge,
+    live, own, pre, pre_node, grad_coarse, from_first, from_second, src, dst, w_in, w_node, w_outs,
+    coarse_out, grad_own, back_first, back_second, sums_out, agg_out, ga_out, pair_node, pair_edge, ga_edge,
 ):
-    halo = jnp.concatenate([from_prev[...], from_next[...]], 0)
+    halo = by_side(from_first, from_second, GROUP)
     table = dot(halo, w_in[:128, :]).astype(BF)
     blocks = range(EC // 128)
     src_rows = src[...]
@@ -296,18 +314,17 @@
     sums_out[...] = src_sums
     ga_edge[...] = ga
     grad_ext = dot_nt(src_sums, w_in[:128, :])
-    back_prev[...] = grad_ext[:SLOT].astype(BF)
-    back_next[...] = grad_ext[SLOT:].astype(BF)
+    back_first[...], back_second[...] = to_mates(grad_ext[:SLOT], grad_ext[SLOT:], GROUP)
     grad_own[...] = grad_total
 
 
 def lift_kernel(
-    own, cot, from_prev, from_next, coarse, grad_part, sums, agg, ga, pair_node, pair_edge,
+    own, cot, from_first, from_second, coarse, grad_part, sums, agg, ga, pair_node, pair_edge,
     ga_edge, src, dst, w_in, refined, pool, w_outs, new_nodes, grads, grad_own,
 ):
     part = 1.0 / 8.0
     rows = own[...]
-    ext = jnp.concatenate([rows, from_prev[...], from_next[...]], 0)
+    ext = jnp.concatenate([rows, by_side(from_first, from_second, GROUP)], 0)
     dst_sums = dot(put(dst[...], range(EC // 128), NC), ga_edge[...]).astype(BF)
     src_sums = dot(put(src[...], range(EC // 128), NC), ga_edge[...]).astype(BF)
     grad_own[...] = (
@@ -326,10 +343,10 @@
 
 
 def prep_kernel(
-    act, act_node, w_outs, src, from_prev, from_next, src_part, src_rows, hidden_out, slope_out, normed_out, inv_out, hidden_node, slope_node,
+    act, act_node, w_outs, src, from_first, from_second, src_part, src_rows, hidden_out, slope_out, normed_out, inv_out, hidden_node, slope_node,
     normed_node, inv_node,
 ):
-    halo = jnp.concatenate([from_prev[...], from_next[...]], 0)
+    halo = by_side(from_first, from_second, EVERY)
     src_cols = columns(src[...] - NF)
     for c in range(EF // 128 // FINE_BLK):
         at = pl.ds(c * FINE_BLK * 128, FINE_BLK * 128)
@@ -350,12 +367,12 @@
 
 
 def fine_back_kernel(
-    lives, counts, grad_own, divisor, ret_prev, ret_next, send, cot, pool, node, agg, src_rows,
+    lives, counts, grad_own, divisor, ret_first, ret_second, send, cot, pool, node, agg, src_rows,
     hidden, slope, normed, inv, hidden_node, slope_node, normed_node, inv_node, dst_rows, edge,
     cot_edges, src, dst, w_in, w_node, w_outs, coarse_grads, grad_new, ga_out, grad_node, ga_node,
-    grads, back_prev, back_next,
+    grads_hbm, back_first, back_second, grads, sems,
 ):
-    back = jnp.concatenate([ret_prev[...], ret_next[...]], 0)
+    back = by_side(ret_first, ret_second, GROUP)
     hot = put(live_slots(send[...], counts, GROUP), (0, 1), NC)
     grad_pool = (grad_own[...] + dot(hot, back)).astype(BF).astype(F32) / divisor[...]
     pooled = dot(pick(columns(pool[...]), range(NF // 128), NC), grad_pool.astype(BF))
@@ -368,6 +385,14 @@
     grads[1280:1408, :] = dot_tn(hidden_node[...], go).astype(BF)
     grad_node[...] = grad_refined.astype(BF)
     ga_node[...] = ga
+    grads[640:1152, :] = coarse_grads[0:512, :]
+    grads[1408:1792, :] = coarse_grads[512:896, :]
+    copies = [
+        pltpu.make_async_copy(grads.at[pl.ds(a, n)], grads_hbm.at[pl.ds(a, n)], sems.at[k])
+        for k, (a, n) in enumerate(((384, 768), (1280, 512), (0, 384), (1152, 128)))
+    ]
+    copies[0].start()
+    copies[1].start()
     dst_cols = columns(live_rows(dst[...], lives[0:1, 0:1]))
     slot_rows = src[...] - NF
     sums = jnp.zeros((2 * SLOT, L), F32)
@@ -385,22 +410,26 @@
         go = norm_back(total, normed[at, :].astype(F32), inv[at, :])
         ga = (dot_nt(go, w_second) * slope[at, :].astype(F32)).astype(BF)
         ga_out[at, :] = ga
-        sums += dot(put(slot_rows, blocks, 2 * SLOT), ga)
         for k, rows in enumerate((edge, src_rows, dst_rows)):
             totals[k] += dot_tn(rows[at, :], ga)
         totals[3] += dot_tn(hidden[at, :], go)
-    sums = dot_nt(sums.astype(BF), w_in[128:256, :])
-    back_prev[...] = sums[:SLOT].astype(BF)
-    back_next[...] = sums[SLOT:].astype(BF)
     for k in range(3):
         grads[k * 128 : (k + 1) * 128, :] = totals[k].astype(BF)
-    grads[640:1152, :] = coarse_grads[0:512, :]
     grads[1152:1280, :] = totals[3].astype(BF)
-    grads[1408:1792, :] = coarse_grads[512:896, :]
+    copies[2].start()
+    copies[3].start()
+    for c in range(EF // 128 // FINE_BLK):
+        blocks = range(c * FINE_BLK, (c + 1) * FINE_BLK)
+        at = pl.ds(c * FINE_BLK * 128, FINE_BLK * 128)
+        sums += dot(put(slot_rows, blocks, 2 * SLOT), ga_out[at, :])
+    sums = dot_nt(sums.astype(BF), w_in[128:256, :])
+    back_first[...], back_second[...] = to_mates(sums[:SLOT], sums[SLOT:], EVERY)
+    for copy in copies:
+        copy.wait()
 
 
 def fine_rest_kernel(
-    counts, grad_new, ga, grad_part, ga_node, src, dst, w_in, w_node, ret_prev, ret_next, send,
+    counts, grad_new, ga, grad_part, ga_node, src, dst, w_in, w_node, ret_first, ret_second, send,
     grad_edges_hbm,
     grad_nodes, grad_edges, sems,
 ):
@@ -419,7 +448,7 @@
         copies[-1].start()
         src_sums += dot(put(src_rows, blocks, NF), rows)
         dst_sums += dot(put(dst_rows, blocks, NF), rows)
-    back = jnp.concatenate([ret_prev[...], ret_next[...]], 0)
+    back = by_side(ret_first, ret_second, EVERY)
     hot = put(live_slots(send[...], counts, EVERY), (0, 1), NF)
     grad_nodes[...] = (
         grad_part[...].astype(F32)
@@ -439,7 +468,7 @@
     return total.astype(BF)
 
 
-def plane_kernel(parts, ret_prev, ret_next, out):
+def plane_kernel(parts, ret_first, ret_second, out):
     total = added(parts)
     for k in range(out.shape[0]):
         out[k] = total
@@ -463,6 +492,15 @@
 def shift(value, axes, step):
     count = lax.axis_size(axes)
     return lax.ppermute(value, axes, [(i, (i + step) % count) for i in range(count)])
+
+
+def swap_mates(first, second, axes):
+    count = lax.axis_size(axes)
+    step = [1 - 2 * (i % 2) for i in range(count)]
+    return (
+        lax.ppermute(first, axes, [(i, i + step[i]) for i in range(count)]),
+        lax.ppermute(second, axes, [(i, (i - step[i]) % count) for i in range(count)]),
+    )
 
 
 def cross(value):
@@ -495,8 +533,8 @@
     lives = call(
         begin_kernel, "begin", shape(8, 128, dtype=I32), (live, clive), 10**10, space=SMEM
     )
-    to_prev, to_next = call(send_kernel, "send", slots, (lives, node, send, counts), 10**10)
-    from_prev, from_next = shift(to_next, EVERY, 1), shift(to_prev, EVERY, -1)
+    to_first, to_second = call(send_kernel, "send", slots, (lives, node, send, counts), 10**10)
+    from_first, from_second = swap_mates(to_first, to_second, EVERY)
     pre, side, src_part, dst_rows = call(
         pre_kernel, "pre", (f32(EF, L), shape(NC + CNT, L), shape(EF, L), shape(EF, L)),
         (node, w_edge, src, dst, edge, pool, cot),
@@ -504,7 +542,7 @@
     new_edges, act, agg, act_node, refined, payload = call(
         fine_kernel, "fine",
         (shape(EF, L), f32(EF, L), shape(NF, L), f32(NF, L), shape(NF, L), shape(2 * NC + CNT, L)),
-        (lives, pre, edge, node, from_prev, from_next, src, dst, w_edge, w_node, w_outs, pool, side),
+        (lives, pre, edge, node, from_first, from_second, src, dst, w_edge, w_node, w_outs, pool, side),
         hbm_out=(0,), scratch=edge_copies,
     )
     total, part = call(
@@ -516,50 +554,51 @@
         prep_kernel, "prep",
         (shape(EF, L), shape(EF, L), shape(EF, L), shape(EF, L), f32(EF, 1),
          shape(NF, L), f32(NF, L), f32(NF, L), f32(NF, 1)),
-        (act, act_node, w_outs, src, from_prev, from_next, src_part),
+        (act, act_node, w_outs, src, from_first, from_second, src_part),
     )
     joined = call(
         join_kernel, "join", shape(2 * NC + CNT, L), (total, near, part, prepared[-1]), 10**6,
         scratch=(pltpu.VMEM((2 * NC + CNT, L), F32),),
     )
-    own, pooled_cot, divisor, to_prev, to_next = call(
+    own, pooled_cot, divisor, to_first, to_second = call(
         pool_kernel, "pool", (shape(NC, L), shape(NC, L), f32(NC, L)) + slots,
         (joined, shift(joined, "c", 1), csend, ccounts), 10**7,
     )
-    cfrom_prev, cfrom_next = shift(to_next, GROUP, 1), shift(to_prev, GROUP, -1)
+    cfrom_first, cfrom_second = swap_mates(to_first, to_second, GROUP)
     cpre, cpre_node, grad_coarse = call(
         coarse_pre_kernel, "coarse_pre", (f32(EC, L), f32(NC, L), shape(NC, L)),
         (own, pooled_cot, csrc, cdst, w_cedge, w_cnode, w_outs),
     )
-    coarse, grad_part, back_prev, back_next, sums, cagg, cga, pair_node, pair_edge, cga_edge = call(
+    coarse, grad_part, back_first, back_second, sums, cagg, cga, pair_node, pair_edge, cga_edge = call(
         coarse_kernel, "coarse",
         (shape(NC, L), f32(NC, L)) + slots
         + (shape(2 * SLOT, L), shape(NC, L), shape(NC, L), shape(2, NC, L),
            shape(2, EC, L), shape(EC, L)),
-        (lives, own, cpre, cpre_node, grad_coarse, cfrom_prev, cfrom_next, csrc, cdst,
+        (lives, own, cpre, cpre_node, grad_coarse, cfrom_first, cfrom_second, csrc, cdst,
          w_cedge, w_cnode, w_outs),
     )
-    cret_prev, cret_next = shift(back_next, GROUP, 1), shift(back_prev, GROUP, -1)
+    cret_first, cret_second = swap_mates(back_first, back_second, GROUP)
     new_nodes, coarse_grads, grad_own = call(
         lift_kernel, "lift", (shape(NF, L), shape(896, L), f32(NC, L)),
-        (own, pooled_cot, cfrom_prev, cfrom_next, coarse, grad_part, sums, cagg, cga, pair_node,
+        (own, pooled_cot, cfrom_first, cfrom_second, coarse, grad_part, sums, cagg, cga, pair_node,
          pair_edge, cga_edge, csrc, cdst, w_cedge, refined, pool, w_outs),
     )
-    grad_new, ga, grad_part, ga_node, grads, back_prev, back_next = call(
+    grad_new, ga, grad_part, ga_node, grads, back_first, back_second = call(
         fine_back_kernel, "fine_back",
         (shape(EF, L), shape(EF, L), shape(NF, L), shape(NF, L), shape(GRADS, L)) + slots,
-        (lives, ccounts, grad_own, divisor, cret_prev, cret_next, csend, cot, pool, node, agg)
+        (lives, ccounts, grad_own, divisor, cret_first, cret_second, csend, cot, pool, node, agg)
         + tuple(prepared)
         + (dst_rows, edge, cot_edges, src, dst, w_edge, w_node, w_outs, coarse_grads),
-    )
-    ret_prev, ret_next = shift(back_next, EVERY, 1), shift(back_prev, EVERY, -1)
+        hbm_out=(4,), scratch=(pltpu.VMEM((GRADS, L), BF), pltpu.SemaphoreType.DMA((4,))),
+    )
+    ret_first, ret_second = swap_mates(back_first, back_second, EVERY)
     parts = exchange(grads.reshape(32, GRADS // 32, L), PLANE)
     spread = call(
-        plane_kernel, "sum_plane", shape(8, GRADS // 32, L), (parts, ret_prev, ret_next), 10**6
+        plane_kernel, "sum_plane", shape(8, GRADS // 32, L), (parts, ret_first, ret_second), 10**6
     )
     grad_edges, grad_nodes = call(
         fine_rest_kernel, "fine_rest", (shape(EF, L), shape(NF, L)),
-        (counts, grad_new, ga, grad_part, ga_node, src, dst, w_edge, w_node, ret_prev, ret_next,
+        (counts, grad_new, ga, grad_part, ga_node, src, dst, w_edge, w_node, ret_first, ret_second,
          send),
         hbm_out=(0,), scratch=edge_copies,
     )

time: 104 us -> 102 us (0.981)
  blocking collectives: 15.9 us -> 13.9 us
    ppermute x0 -> x8, starting transfers between devices: none -> 16 us  [the longest x4 11.9 us: swap_mates(): lax.ppermute(second, axes, [(i, (i - step[i]) % count) for i in range(cou...]
    ppermute x11 -> x3, starting transfers between devices: 27.1 us -> 11.1 us  [shift(): lax.ppermute(value, axes, [(i, (i + step) % count) for i in range(count)])]
    ppermute x11 -> x3, waiting for transfers between devices: 10 us -> 4.58 us  [shift(): lax.ppermute(value, axes, [(i, (i + step) % count) for i in range(count)])]
    ppermute x0 -> x8, waiting for transfers between devices: none -> 4.04 us  [the longest x4 4.03 us: swap_mates(): lax.ppermute(second, axes, [(i, (i - step[i]) % count) for i in range(cou...]
    all_to_all x1, blocking collectives: 15.9 us -> 13.9 us  [exchange(): return lax.all_to_all(value, axes, 0, 0)]
    all_to_all x2, waiting for transfers between devices: 12.3 us -> 14.2 us  [exchange(): return lax.all_to_all(value, axes, 0, 0)]
  transfers between devices with their start and end apart: 14 -> 14, of which waited for: 9 -> 8; matrix products, arithmetic and copies ran while one was open for 0% -> 0% of each run, Pallas kernels for 10% -> 10%
where the time goes in v2:
time: 102 us
  starting transfers between devices  37.4 us (37%)
  Pallas kernels  24.7 us (24%)
  waiting for transfers between devices  22.9 us (22%)
  blocking collectives  13.9 us (14%)
  between operations  2.25 us (2%)
    pallas_call x16, Pallas kernels, call(): pl.pallas_call(kernel, name=name, out_shape=out_shape, in_specs=[space] *...  24.7 us
    all_to_all x2, waiting for transfers between devices, exchange(): return lax.all_to_all(value, axes, 0, 0)  14.2 us
    all_to_all x1, blocking collectives, exchange(): return lax.all_to_all(value, axes, 0, 0)  13.9 us
    ppermute x4, starting transfers between devices, swap_mates(): lax.ppermute(second, axes, [(i, (i - step[i]) % count) for i in range(cou...  11.9 us
    ppermute x3, starting transfers between devices, shift(): lax.ppermute(value, axes, [(i, (i + step) % count) for i in range(count)])  11.1 us
    all_to_all x2, starting transfers between devices, exchange(): return lax.all_to_all(value, axes, 0, 0)  10.3 us
    ppermute x3, waiting for transfers between devices, shift(): lax.ppermute(value, axes, [(i, (i + step) % count) for i in range(count)])  4.58 us
    ppermute x4, starting transfers between devices, swap_mates(): lax.ppermute(first, axes, [(i, i + step[i]) for i in range(count)])  4.13 us
  transfers between devices with their start and end apart: 14, of which 8 were waited for; matrix products, arithmetic and copies ran while one was open for 0% of the time, Pallas kernels for 10%

profile of v2, /device:TPU:1, one launch (start us, length us, event | category | flops | bytes accessed | tf_op | source)
XLA Modules:
  0.0 102.1 jit_solution(7661545572075529621)
XLA Ops:
  1.9 0.0 copy-start.3
  1.9 0.0 copy-start.16
  2.0 0.0 copy-start.17
  2.0 0.9 copy-done.3
  2.8 0.0 copy-done.16
  2.9 0.0 copy-start.5
  2.9 0.0 copy-start.7
  2.9 0.0 copy-start.8
  2.9 0.0 copy-start.10
  2.9 0.4 send.1
  3.3 3.3 %collective-permute-start = (bf16[128,128]{1,0:T(8,128)(2,1)S(1)}, bf16[128,128]{1,0:T(8,128)(2,1)S(1)}, u32[]{:S(2)}, u32[]{:S(2)}) collective-permute-start(bf16[128,128]{1,0:T(8,128)(2,1)S(1)} %get-tuple-element.68), channel_id=1, source_target_pairs={{0,1},{1,0},{2,3},{3,2},{4,5},{5,4},{6,7},{7,6},{8,9},{9,8},{10,11... | collective-permute-start | bytes 98312 | tf_op jit(solution)/shard_map/ppermute | solution.py:501
  6.7 0.0 collective-permute-start.1
  6.7 0.0 copy-start.2
  6.7 0.0 copy-start.6
  6.7 2.3 %pre.1 = (f32[3072,128]{1,0:T(8,128)S(1)}, bf16[272,128]{1,0:T(8,128)(2,1)S(1)}, bf16[3072,128]{1,0:T(8,128)(2,1)S(1)}, bf16[3072,128]{1,0:T(8,128)(2,1)S(1)}) custom-call(bf16[512,128]{1,0:T(8,128)(2,1)S(1)} %copy-done.3, bf16[384,128]{1,0:T(8,128)(2,1)S(1)} %copy-done.5, s32[24,128]{1,0:T(8,128)S(1)} %bitcast.10, s32[24,128]{1,0:T(8,128)S(1)} %bitcast.15, ...), custom_call_target="tpu_custom_call" | custom-call | flops 1000000000 | bytes 1173504 | tf_op jit(solution)/shard_map/pre/pallas_call | solution.py:42
  9.1 0.0 collective-permute-done.from_first
  9.1 0.9 collective-permute-done.1.from_second
  10.0 3.9 %fine.1 = (bf16[3072,128]{1,0:T(8,128)(2,1)}, f32[3072,128]{1,0:T(8,128)S(1)}, bf16[512,128]{1,0:T(8,128)(2,1)S(1)}, f32[512,128]{1,0:T(8,128)S(1)}, bf16[512,12...) custom-call(s32[8,128]{1,0:T(8,128)S(1)} %begin.1.lives.live, f32[3072,128]{1,0:T(8,128)S(1)} %get-tuple-element.67.pre, ...), custom_call_target="tpu_custom_call" | custom-call | flops 1000000000 | bytes 2983936 | tf_op jit(solution)/shard_map/fine/pallas_call | solution.py:42
  13.9 8.1 %collective-permute-start.2 = (bf16[528,128]{1,0:T(8,128)(2,1)S(1)}, bf16[528,128]{1,0:T(8,128)(2,1)S(1)}, u32[]{:S(2)}, u32[]{:S(2)}) collective-permute-start(bf16[528,128]{1,0:T(8,128)(2,1)S(1)} %get-tuple-element.71.a), channel_id=1, source_target_pairs={{0,1},{1,0},{2,3},{3,2},{4,5},{5,4},{6,7},{7,6},{8,9},{9,8},{10,11... | collective-permute-start | bytes 405512 | tf_op jit(solution)/shard_map/ppermute | solution.py:494
  22.0 1.0 collective-permute-done.2.b
  23.0 0.1 pair.1
  23.0 0.1 collective-permute-start.3
  23.1 0.1 collective-permute-start.4
  23.2 0.0 copy-start.9
  23.2 0.0 copy-start.11
  23.3 0.0 copy-start.12
  23.3 0.0 copy-start.13
  23.3 0.0 copy-start.14
  23.3 0.0 copy-start.15
  23.3 2.0 %prep.1 = (bf16[3072,128]{1,0:T(8,128)(2,1)S(1)}, bf16[3072,128]{1,0:T(8,128)(2,1)S(1)}, bf16[3072,128]{1,0:T(8,128)(2,1)S(1)}, bf16[3072,128]{1,0:T(8,128)(2,1)...) custom-call(f32[3072,128]{1,0:T(8,128)S(1)} %get-tuple-element.74.ac, ...), custom_call_target="tpu_custom_call" | custom-call | flops 1000000000 | bytes 2863104 | tf_op jit(solution)/shard_map/prep/pallas_call | solution.py:42
  25.3 2.6 %collective-permute-done.4.part = bf16[272,128]{1,0:T(8,128)(2,1)S(1)} collective-permute-done((bf16[272,128]{1,0:T(8,128)(2,1)S(1)}, bf16[272,128]{1,0:T(8,128)(2,1)S(1)}, u32[]{:S(2)}, u32[]{:S(2)}) %collective-permute-start.4) | collective-permute-done | bytes 69664 | tf_op jit(solution)/shard_map/ppermute | solution.py:494
  27.9 0.0 collective-permute-done.3.near
  27.9 0.1 join.1.a
  28.0 2.9 %collective-permute-start.5 = (bf16[528,128]{1,0:T(8,128)(2,1)S(1)}, bf16[528,128]{1,0:T(8,128)(2,1)S(1)}, u32[]{:S(2)}, u32[]{:S(2)}) collective-permute-start(bf16[528,128]{1,0:T(8,128)(2,1)S(1)} %join.1.a), channel_id=1, source_target_pairs={{0,1},{1,0},{2,3},{3,2},{4,5},{5,4},{6,7},{7,6},{8,9},{9,8},{10,11... | collective-permute-start | bytes 405512 | tf_op jit(solution)/shard_map/ppermute | solution.py:494
  31.0 1.0 collective-permute-done.5.b
  31.9 0.0 copy-done.9
  32.0 0.4 pool.1
  32.4 0.3 collective-permute-start.6
  32.7 5.4 %collective-permute-start.7 = (bf16[128,128]{1,0:T(8,128)(2,1)S(1)}, bf16[128,128]{1,0:T(8,128)(2,1)S(1)}, u32[]{:S(2)}, u32[]{:S(2)}) collective-permute-start(bf16[128,128]{1,0:T(8,128)(2,1)S(1)} %get-tuple-element.81), channel_id=1, source_target_pairs={{0,248},{8,16},{16,8},{24,32},{32,24},{40,48},{48,40},{56,64},{64,... | collective-permute-start | bytes 98312 | tf_op jit(solution)/shard_map/ppermute | solution.py:502
  38.1 0.0 copy-done.14
  38.1 0.9 coarse_pre.1
  39.0 0.0 collective-permute-done.6.from_first
  39.0 0.4 collective-permute-done.7.from_second
  39.4 3.1 %coarse.1 = (bf16[256,128]{1,0:T(8,128)(2,1)S(1)}, f32[256,128]{1,0:T(8,128)S(1)}, bf16[128,128]{1,0:T(8,128)(2,1)S(1)}, bf16[128,128]{1,0:T(8,128)(2,1)S(1)}, b...) custom-call(s32[8,128]{1,0:T(8,128)S(1)} %begin.1.lives.live, ...), custom_call_target="tpu_custom_call" | custom-call | flops 1000000000 | bytes 1425408 | tf_op jit(solution)/shard_map/coarse/pallas_call | solution.py:42
  42.5 0.1 collective-permute-start.8
  42.6 4.9 %collective-permute-start.9 = (bf16[128,128]{1,0:T(8,128)(2,1)S(1)}, bf16[128,128]{1,0:T(8,128)(2,1)S(1)}, u32[]{:S(2)}, u32[]{:S(2)}) collective-permute-start(bf16[128,128]{1,0:T(8,128)(2,1)S(1)} %get-tuple-element.99), channel_id=1, source_target_pairs={{0,248},{8,16},{16,8},{24,32},{32,24},{40,48},{48,40},{56,64},{64,... | collective-permute-start | bytes 98312 | tf_op jit(solution)/shard_map/ppermute | solution.py:502
  47.5 1.5 %lift.1 = (bf16[512,128]{1,0:T(8,128)(2,1)}, bf16[896,128]{1,0:T(8,128)(2,1)S(1)}, f32[256,128]{1,0:T(8,128)S(1)}) custom-call(bf16[256,128]{1,0:T(8,128)(2,1)S(1)} %get-tuple-element.78.own, bf16[256,128]{1,0:T(8,128)(2,1)S(1)} %get-tuple-element.79.cot, bf16[128,128]{1,0:T(8,128)(2,1)S(1)} %collective-permute-done.6.from_first, ...), custom_call_target="tpu_custom_call" | custom-call | flops 1000000000 | bytes 2275328 | tf_op jit(solution)/shard_map/lift/pallas_call | solution.py:42
  49.0 0.0 collective-permute-done.8.ret_first
  49.0 0.0 collective-permute-done.9.ret_second
  49.0 0.0 copy-done.1
  49.0 4.8 %fine_back.1 = (bf16[3072,128]{1,0:T(8,128)(2,1)S(1)}, bf16[3072,128]{1,0:T(8,128)(2,1)S(1)}, bf16[512,128]{1,0:T(8,128)(2,1)S(1)}, bf16[512,128]{1,0:T(8,128)(2...) custom-call(s32[8,128]{1,0:T(8,128)S(1)} %begin.1.lives.live, ...), custom_call_target="tpu_custom_call" | custom-call | flops 1000000000 | bytes 7484424 | tf_op jit(solution)/shard_map/fine_back/pallas_call | solution.py:42
  53.8 5.7 %all-to-all-start = ((bf16[32,56,128]{2,1,0:T(8,128)(2,1)}), bf16[32,56,128]{2,1,0:T(8,128)(2,1)S(1)}, u32[]{:S(2)}, u32[]{:S(2)}) async-start(bf16[32,56,128]{2,1,0:T(8,128)(2,1)} %bitcast.7), calls=%async_computation | async-start | bytes 917504 | tf_op jit(solution)/shard_map/all_to_all | solution.py:518
  59.5 0.4 collective-permute-start.10
  59.9 1.6 %collective-permute-start.11 = (bf16[128,128]{1,0:T(8,128)(2,1)S(1)}, bf16[128,128]{1,0:T(8,128)(2,1)S(1)}, u32[]{:S(2)}, u32[]{:S(2)}) collective-permute-start(bf16[128,128]{1,0:T(8,128)(2,1)S(1)} %get-tuple-element.116), channel_id=1, source_target_pairs={{0,255},{1,2},{2,1},{3,4},{4,3},{5,6},{6,5},{7,8},{8,7},{9,10},{10... | collective-permute-start | bytes 98312 | tf_op jit(solution)/shard_map/ppermute | solution.py:502
  61.5 0.0 collective-permute-done.10.ret_first
  61.5 2.7 %collective-permute-done.11.ret_second = bf16[128,128]{1,0:T(8,128)(2,1)S(1)} collective-permute-done((bf16[128,128]{1,0:T(8,128)(2,1)S(1)}, bf16[128,128]{1,0:T(8,128)(2,1)S(1)}, u32[]{:S(2)}, u32[]{:S(2)}) %collective-permute-start.11) | collective-permute-done | bytes 32800 | tf_op jit(solution)/shard_map/ppermute | solution.py:502
  64.3 6.4 %all-to-all-done.parts = bf16[32,56,128]{2,1,0:T(8,128)(2,1)S(1)} async-done(((bf16[32,56,128]{2,1,0:T(8,128)(2,1)}), bf16[32,56,128]{2,1,0:T(8,128)(2,1)S(1)}, u32[]{:S(2)}, u32[]{:S(2)}) %all-to-all-start) | async-done | bytes 458784 | tf_op jit(solution)/shard_map/all_to_all | solution.py:518
  70.7 0.1 sum_plane.1
  70.8 13.9 %all_to_all.15.parts = bf16[8,56,128]{2,1,0:T(8,128)(2,1)S(1)} all-to-all(bf16[8,56,128]{2,1,0:T(8,128)(2,1)S(1)} %sum_plane.1), channel_id=1, replica_groups=mesh['z'=8,'x'=4,'y'=4,'c'=2] {'z'}, dimensions={0} | all-to-all | bytes 229376 | tf_op jit(solution)/shard_map/all_to_all | solution.py:518
  84.7 0.8 sum_z.1
  85.5 4.6 %all-to-all-start.2 = ((bf16[32,56,128]{2,1,0:T(8,128)(2,1)}), bf16[32,56,128]{2,1,0:T(8,128)(2,1)S(1)}, u32[]{:S(2)}, u32[]{:S(2)}) async-start(bf16[32,56,128]{2,1,0:T(8,128)(2,1)} %sum_z.1), calls=%async_computation.2 | async-start | bytes 917504 | tf_op jit(solution)/shard_map/all_to_all | solution.py:518
  90.0 3.3 %fine_rest.1 = (bf16[3072,128]{1,0:T(8,128)(2,1)}, bf16[512,128]{1,0:T(8,128)(2,1)}) custom-call(s32[1,2]{1,0:T(1,128)S(1)} %copy-done.17, bf16[3072,128]{1,0:T(8,128)(2,1)S(1)} %get-tuple-element.111.grad_new, bf16[3072,128]{1,0:T(8,128)(2,1)S(1)} %get-tuple-element.112.ga, bf16[512,128]{1,0:T(8,128)(2,1)S(1)} %get-tuple-element.113.grad_part, ...), custom_call_target="tpu_custom_call" | custom-call | flops 1000000000 | bytes 2089992 | tf_op jit(solution)/shard_map/fine_rest/pallas_call | solution.py:42
  93.3 7.8 %all-to-all-done.2 = bf16[32,56,128]{2,1,0:T(8,128)(2,1)S(1)} async-done(((bf16[32,56,128]{2,1,0:T(8,128)(2,1)}), bf16[32,56,128]{2,1,0:T(8,128)(2,1)S(1)}, u32[]{:S(2)}, u32[]{:S(2)}) %all-to-all-start.2) | async-done | bytes 458784 | tf_op jit(solution)/shard_map/all_to_all | solution.py:518
  101.1 1.0 end.1
  (17 shorter events, 0.0 us)
Async XLA Ops:
  1.9 0.9 copy-start.3
  1.9 0.9 copy-start.16
  2.0 0.9 copy-start.17
  2.8 3.8 %copy-start = (bf16[3072,128]{1,0:T(8,128)(2,1)S(1)}, bf16[3072,128]{1,0:T(8,128)(2,1)}, u32[]{:S(2)}) copy-start(bf16[3072,128]{1,0:T(8,128)(2,1)} %edge.5) | copy-start | bytes 2359300
  2.8 3.8 %copy-start.4 = (bf16[512,128]{1,0:T(8,128)(2,1)S(1)}, bf16[512,128]{1,0:T(8,128)(2,1)}, u32[]{:S(2)}) copy-start(bf16[512,128]{1,0:T(8,128)(2,1)} %cot.3) | copy-start | bytes 393220
  2.9 3.8 %copy-start.5 = (bf16[384,128]{1,0:T(8,128)(2,1)S(1)}, bf16[384,128]{1,0:T(8,128)(2,1)}, u32[]{:S(2)}) copy-start(bf16[384,128]{1,0:T(8,128)(2,1)} %w_in.13) | copy-start | bytes 294916
  2.9 3.8 %copy-start.7 = (s32[3072]{0:T(1024)S(1)}, s32[3072]{0:T(1024)}, u32[]{:S(2)}) copy-start(s32[3072]{0:T(1024)} %param.22) | copy-start | bytes 36868
  2.9 3.8 %copy-start.8 = (s32[3072]{0:T(1024)S(1)}, s32[3072]{0:T(1024)}, u32[]{:S(2)}) copy-start(s32[3072]{0:T(1024)} %param.23) | copy-start | bytes 36868
  2.9 3.8 %copy-start.10 = (s32[512]{0:T(512)S(1)}, s32[512]{0:T(512)}, u32[]{:S(2)}) copy-start(s32[512]{0:T(512)} %param.27) | copy-start | bytes 6148
  3.3 5.8 %collective-permute-start = (bf16[128,128]{1,0:T(8,128)(2,1)S(1)}, bf16[128,128]{1,0:T(8,128)(2,1)S(1)}, u32[]{:S(2)}, u32[]{:S(2)}) collective-permute-start(bf16[128,128]{1,0:T(8,128)(2,1)S(1)} %get-tuple-element.68), channel_id=1, source_target_pairs={{0,1},{1,0},{2,3},{3,2},{4,5},{5,4},{6,7},{7,6},{8,9},{9,8},{10,11... | collective-permute-start | bytes 98312 | tf_op jit(solution)/shard_map/ppermute | solution.py:501
  6.7 3.3 %collective-permute-start.1 = (bf16[128,128]{1,0:T(8,128)(2,1)S(1)}, bf16[128,128]{1,0:T(8,128)(2,1)S(1)}, u32[]{:S(2)}, u32[]{:S(2)}) collective-permute-start(bf16[128,128]{1,0:T(8,128)(2,1)S(1)} %get-tuple-element.69), channel_id=1, source_target_pairs={{0,255},{1,2},{2,1},{3,4},{4,3},{5,6},{6,5},{7,8},{8,7},{9,10},{10... | collective-permute-start | bytes 98312 | tf_op jit(solution)/shard_map/ppermute | solution.py:502
  6.7 3.3 %copy-start.2 = (bf16[5,128,128]{2,1,0:T(8,128)(2,1)S(1)}, bf16[5,128,128]{2,1,0:T(8,128)(2,1)}, u32[]{:S(2)}) copy-start(bf16[5,128,128]{2,1,0:T(8,128)(2,1)} %w_outs.11) | copy-start | bytes 491524
  6.7 3.3 %copy-start.6 = (bf16[256,128]{1,0:T(8,128)(2,1)S(1)}, bf16[256,128]{1,0:T(8,128)(2,1)}, u32[]{:S(2)}) copy-start(bf16[256,128]{1,0:T(8,128)(2,1)} %w_node.9) | copy-start | bytes 196612
  13.9 9.1 %collective-permute-start.2 = (bf16[528,128]{1,0:T(8,128)(2,1)S(1)}, bf16[528,128]{1,0:T(8,128)(2,1)S(1)}, u32[]{:S(2)}, u32[]{:S(2)}) collective-permute-start(bf16[528,128]{1,0:T(8,128)(2,1)S(1)} %get-tuple-element.71.a), channel_id=1, source_target_pairs={{0,1},{1,0},{2,3},{3,2},{4,5},{5,4},{6,7},{7,6},{8,9},{9,8},{10,11... | collective-permute-start | bytes 405512 | tf_op jit(solution)/shard_map/ppermute | solution.py:494
  23.0 4.9 %collective-permute-start.3 = (bf16[528,128]{1,0:T(8,128)(2,1)S(1)}, bf16[528,128]{1,0:T(8,128)(2,1)S(1)}, u32[]{:S(2)}, u32[]{:S(2)}) collective-permute-start(bf16[528,128]{1,0:T(8,128)(2,1)S(1)} %get-tuple-element.72.own), channel_id=1, source_target_pairs={{0,2},{1,7},{2,4},{3,1},{4,6},{5,3},{6,0},{7,5},{8,10},{9,15},{10,... | collective-permute-start | bytes 405512 | tf_op jit(solution)/shard_map/ppermute | solution.py:514
  23.1 4.8 %collective-permute-start.4 = (bf16[272,128]{1,0:T(8,128)(2,1)S(1)}, bf16[272,128]{1,0:T(8,128)(2,1)S(1)}, u32[]{:S(2)}, u32[]{:S(2)}) collective-permute-start(bf16[272,128]{1,0:T(8,128)(2,1)S(1)} %get-tuple-element.73), channel_id=1, source_target_pairs={{0,4},{2,6},{4,0},{6,2},{1,5},{3,7},{5,1},{7,3},{8,12},{10,14},{12... | collective-permute-start | bytes 208904 | tf_op jit(solution)/shard_map/ppermute | solution.py:494
  23.2 8.7 %copy-start.9 = (s32[1,2,128]{2,1,0:T(2,128)S(1)}, s32[1,2,128]{2,1,0:T(2,128)}, u32[]{:S(2)}) copy-start(s32[1,2,128]{2,1,0:T(2,128)} %param.31) | copy-start | bytes 3076
  23.2 8.7 %copy-start.11 = (s32[1,2]{1,0:T(1,128)S(1)}, s32[1,2]{1,0:T(1,128)}, u32[]{:S(2)}) copy-start(s32[1,2]{1,0:T(1,128)} %counts.6) | copy-start | bytes 28
  23.3 14.8 %copy-start.12 = (bf16[256,128]{1,0:T(8,128)(2,1)S(1)}, bf16[256,128]{1,0:T(8,128)(2,1)}, u32[]{:S(2)}) copy-start(bf16[256,128]{1,0:T(8,128)(2,1)} %w_node.7) | copy-start | bytes 196612
  23.3 14.8 %copy-start.13 = (bf16[256,128]{1,0:T(8,128)(2,1)S(1)}, bf16[256,128]{1,0:T(8,128)(2,1)}, u32[]{:S(2)}) copy-start(bf16[256,128]{1,0:T(8,128)(2,1)} %w_in.11) | copy-start | bytes 196612
  23.3 14.8 %copy-start.14 = (s32[1536]{0:T(1024)S(1)}, s32[1536]{0:T(1024)}, u32[]{:S(2)}) copy-start(s32[1536]{0:T(1024)} %param.28) | copy-start | bytes 18436
  23.3 14.8 %copy-start.15 = (s32[1536]{0:T(1024)S(1)}, s32[1536]{0:T(1024)}, u32[]{:S(2)}) copy-start(s32[1536]{0:T(1024)} %param.29) | copy-start | bytes 18436
  28.0 3.9 %collective-permute-start.5 = (bf16[528,128]{1,0:T(8,128)(2,1)S(1)}, bf16[528,128]{1,0:T(8,128)(2,1)S(1)}, u32[]{:S(2)}, u32[]{:S(2)}) collective-permute-start(bf16[528,128]{1,0:T(8,128)(2,1)S(1)} %join.1.a), channel_id=1, source_target_pairs={{0,1},{1,0},{2,3},{3,2},{4,5},{5,4},{6,7},{7,6},{8,9},{9,8},{10,11... | collective-permute-start | bytes 405512 | tf_op jit(solution)/shard_map/ppermute | solution.py:494
  32.4 6.6 %collective-permute-start.6 = (bf16[128,128]{1,0:T(8,128)(2,1)S(1)}, bf16[128,128]{1,0:T(8,128)(2,1)S(1)}, u32[]{:S(2)}, u32[]{:S(2)}) collective-permute-start(bf16[128,128]{1,0:T(8,128)(2,1)S(1)} %get-tuple-element.80), channel_id=1, source_target_pairs={{0,8},{8,0},{16,24},{24,16},{32,40},{40,32},{48,56},{56,48},{64,72... | collective-permute-start | bytes 98312 | tf_op jit(solution)/shard_map/ppermute | solution.py:501
  32.7 6.7 %collective-permute-start.7 = (bf16[128,128]{1,0:T(8,128)(2,1)S(1)}, bf16[128,128]{1,0:T(8,128)(2,1)S(1)}, u32[]{:S(2)}, u32[]{:S(2)}) collective-permute-start(bf16[128,128]{1,0:T(8,128)(2,1)S(1)} %get-tuple-element.81), channel_id=1, source_target_pairs={{0,248},{8,16},{16,8},{24,32},{32,24},{40,48},{48,40},{56,64},{64,... | collective-permute-start | bytes 98312 | tf_op jit(solution)/shard_map/ppermute | solution.py:502
  42.5 6.5 %collective-permute-start.8 = (bf16[128,128]{1,0:T(8,128)(2,1)S(1)}, bf16[128,128]{1,0:T(8,128)(2,1)S(1)}, u32[]{:S(2)}, u32[]{:S(2)}) collective-permute-start(bf16[128,128]{1,0:T(8,128)(2,1)S(1)} %get-tuple-element.98), channel_id=1, source_target_pairs={{0,8},{8,0},{16,24},{24,16},{32,40},{40,32},{48,56},{56,48},{64,72... | collective-permute-start | bytes 98312 | tf_op jit(solution)/shard_map/ppermute | solution.py:501
  42.6 6.4 %collective-permute-start.9 = (bf16[128,128]{1,0:T(8,128)(2,1)S(1)}, bf16[128,128]{1,0:T(8,128)(2,1)S(1)}, u32[]{:S(2)}, u32[]{:S(2)}) collective-permute-start(bf16[128,128]{1,0:T(8,128)(2,1)S(1)} %get-tuple-element.99), channel_id=1, source_target_pairs={{0,248},{8,16},{16,8},{24,32},{32,24},{40,48},{48,40},{56,64},{64,... | collective-permute-start | bytes 98312 | tf_op jit(solution)/shard_map/ppermute | solution.py:502
  47.5 1.5 %copy-start.1 = (bf16[3072,128]{1,0:T(8,128)(2,1)S(1)}, bf16[3072,128]{1,0:T(8,128)(2,1)}, u32[]{:S(2)}) copy-start(bf16[3072,128]{1,0:T(8,128)(2,1)} %cot_edges.1) | copy-start | bytes 2359300
  53.8 16.9 %all-to-all-start = ((bf16[32,56,128]{2,1,0:T(8,128)(2,1)}), bf16[32,56,128]{2,1,0:T(8,128)(2,1)S(1)}, u32[]{:S(2)}, u32[]{:S(2)}) async-start(bf16[32,56,128]{2,1,0:T(8,128)(2,1)} %bitcast.7), calls=%async_computation | async-start | bytes 917504 | tf_op jit(solution)/shard_map/all_to_all | solution.py:518
  59.5 2.0 %collective-permute-start.10 = (bf16[128,128]{1,0:T(8,128)(2,1)S(1)}, bf16[128,128]{1,0:T(8,128)(2,1)S(1)}, u32[]{:S(2)}, u32[]{:S(2)}) collective-permute-start(bf16[128,128]{1,0:T(8,128)(2,1)S(1)} %get-tuple-element.115), channel_id=1, source_target_pairs={{0,1},{1,0},{2,3},{3,2},{4,5},{5,4},{6,7},{7,6},{8,9},{9,8},{10,11... | collective-permute-start | bytes 98312 | tf_op jit(solution)/shard_map/ppermute | solution.py:501
  59.9 4.3 %collective-permute-start.11 = (bf16[128,128]{1,0:T(8,128)(2,1)S(1)}, bf16[128,128]{1,0:T(8,128)(2,1)S(1)}, u32[]{:S(2)}, u32[]{:S(2)}) collective-permute-start(bf16[128,128]{1,0:T(8,128)(2,1)S(1)} %get-tuple-element.116), channel_id=1, source_target_pairs={{0,255},{1,2},{2,1},{3,4},{4,3},{5,6},{6,5},{7,8},{8,7},{9,10},{10... | collective-permute-start | bytes 98312 | tf_op jit(solution)/shard_map/ppermute | solution.py:502
  85.5 15.7 %all-to-all-start.2 = ((bf16[32,56,128]{2,1,0:T(8,128)(2,1)}), bf16[32,56,128]{2,1,0:T(8,128)(2,1)S(1)}, u32[]{:S(2)}, u32[]{:S(2)}) async-start(bf16[32,56,128]{2,1,0:T(8,128)(2,1)} %sum_z.1), calls=%async_computation.2 | async-start | bytes 917504 | tf_op jit(solution)/shard_map/all_to_all | solution.py:518
